TPU v7x, 32 devices: a whole 2x2x4 slice. The times are simulated.
32 devices in a mesh: section: 2 (over core), dp: 16 (over z, y, x).
Axes of the slice: x: 2, y: 2, z: 4, core: 2. Of those that a mesh axis runs over, the one named last changes fastest.
Arguments:
- inputs: bfloat16 [2, 16, 1024, 1024], P(None, 'dp'), may hold values from -6 to 6
- cotangent: bfloat16 [2, 16, 1024, 1024], P(None, 'dp'), may hold values from -6 to 6
- doc_lengths: int32 [2, 16, 8], P(None, 'dp'), may hold values from 1 to 512, 1024 in all within a row
- attend_gain: bfloat16 [2, 1024], P('section'), may hold values from 0.5 to 1.5
- attend_bias: bfloat16 [2, 1024], P('section'), may hold values from -1.796875 to 1.796875
- mixing_weight: bfloat16 [2, 1024, 3072], P('section'), may hold values from -0.1875 to 0.1875
- mixing_bias: bfloat16 [2, 3072], P('section'), may hold values from -1.796875 to 1.796875
- output_weight: bfloat16 [2, 1024, 1024], P('section'), may hold values from -0.75 to 0.75
- output_bias: bfloat16 [2, 1024], P('section'), may hold values from -1.796875 to 1.796875
- feed_gain: bfloat16 [2, 1024], P('section'), may hold values from 0.5 to 1.5
- feed_bias: bfloat16 [2, 1024], P('section'), may hold values from -1.796875 to 1.796875
- expand_weight: bfloat16 [2, 1024, 4096], P('section'), may hold values from -0.1875 to 0.1875
- expand_bias: bfloat16 [2, 4096], P('section'), may hold values from -1.796875 to 1.796875
- reduce_weight: bfloat16 [2, 4096, 1024], P('section'), may hold values from -0.1875 to 0.1875
- reduce_bias: bfloat16 [2, 1024], P('section'), may hold values from -1.796875 to 1.796875
- prefix_embed: bfloat16 [10, 1024], replicated, may hold values from -6 to 6
- hidden_weight: bfloat16 [1024, 512], replicated, may hold values from -0.1875 to 0.1875
- hidden_bias: bfloat16 [512], replicated, may hold values from -3 to 3
- prefix_weight: bfloat16 [2, 512, 2048], P('section', None, 'dp'), may hold values from -0.5 to 0.5
- prefix_bias: bfloat16 [2, 2048], P('section', 'dp'), may hold values from -1.796875 to 1.796875
Outputs:
- layer_out: bfloat16 [2, 2, 16, 1024, 1024], P('section', None, 'dp')
- input_grad: bfloat16 [2, 2, 16, 1024, 1024], P('section', None, 'dp')
- grad_embed: float32 [10, 1024], replicated
- grad_hidden_weight: float32 [1024, 512], replicated
- grad_hidden_bias: float32 [512], replicated
- grad_prefix_weight: float32 [2, 512, 2048], P('section', None, 'dp')
- grad_prefix_bias: float32 [2, 2048], P('section', 'dp')
Inputs may be any that keep to these rules, and one draw needn't show every extreme that they name: `doc_lengths`: each sequence's 8 lengths sum to 1024; the longest of them is exactly 512.
All inputs are finite; a program needn't handle non-finite values.
Results may differ from a plain program's by a relative error of at most 0.018.
Values may be sent and summed in bfloat16 or wider, within the bound.
No kernel may reach another device: no remote copies, remote signals or barrier semaphores. Data moves between devices by JAX's collectives and lax.ppermute only.
A program may use at most 320 MiB of HBM per device.

v0:
```python
import jax
import jax.numpy as jnp
from jax import lax
from jax.sharding import PartitionSpec as P

HEADS = 16
HEAD_DIM = 64
PRE = 10
LENGTH = 1024
BLOCK = 512
MICRO = 2


masked_score = -1000000000.0


def from_behind(block, axis, distance):
    devices = range(lax.axis_size(axis))
    route = [(i - distance, i) for i in devices if i - distance in devices]
    return lax.ppermute(block, axis, route)


def norm_apply(values, gain, offset):
    centre = jnp.mean(values, axis=-1, keepdims=True)
    shifted = values - centre
    variance = jnp.mean(shifted * shifted, axis=-1, keepdims=True)
    return shifted * lax.rsqrt(variance + 1e-05) * gain + offset


def gelu_tanh(values):
    return jax.nn.gelu(values, approximate=True)


def contract_last(left, right):
    return lax.dot_general(
        left, right, (((1,), (1,)), ((), ())), preferred_element_type=jnp.float32
    )


def document_ids(lengths):
    doc_ends = jnp.cumsum(lengths, axis=-1)[..., :-1]
    places = jnp.arange(LENGTH, dtype=jnp.int32)
    return jnp.sum((places[:, None] >= doc_ends[..., None, :]).astype(jnp.int32), axis=-1)


def visibility(doc_ids, start_row, limit):
    places = start_row + jnp.arange(BLOCK, dtype=jnp.int32)
    columns = jnp.arange(limit, dtype=jnp.int32)
    inside = (columns[None, :] <= places[:, None]) & (
        doc_ids[None, :limit] == doc_ids[start_row:limit][:, None]
    )
    return jnp.concatenate([jnp.ones((BLOCK, PRE), dtype=jnp.bool_), inside], 1)


def attend_forward(queries, key_part, value_part, prefix_keys, prefix_values, doc_ids):
    score_scale = HEAD_DIM ** (-0.5)
    all_keys = jnp.concatenate([prefix_keys, key_part], 0).reshape(-1, HEADS, HEAD_DIM)
    all_values = jnp.concatenate([prefix_values, value_part], 0).reshape(-1, HEADS, HEAD_DIM)
    results = []
    totals = []
    for block_index in range(LENGTH // BLOCK):
        start_row = block_index * BLOCK
        limit = start_row + BLOCK
        query_rows = queries[start_row:limit].reshape(BLOCK, HEADS, HEAD_DIM)
        scores = (
            jnp.einsum(
                "qhd,khd->hqk",
                query_rows,
                all_keys[: PRE + limit],
                preferred_element_type=jnp.float32,
            )
            * score_scale
        )
        scores = jnp.where(visibility(doc_ids, start_row, limit)[None], scores, masked_score)
        log_total = jax.nn.logsumexp(scores, axis=-1)
        weights_low = jnp.exp(scores - log_total[..., None]).astype(jnp.bfloat16)
        attended = jnp.einsum(
            "hqk,khd->qhd",
            weights_low,
            all_values[: PRE + limit],
            preferred_element_type=jnp.float32,
        )
        results.append(attended.reshape(BLOCK, HEADS * HEAD_DIM))
        totals.append(log_total)
    return (jnp.concatenate(results, 0), jnp.concatenate(totals, 1))


def attend_backward(
    queries, key_part, value_part, prefix_keys, prefix_values, doc_ids, totals, grad_out
):
    score_scale = HEAD_DIM ** (-0.5)
    all_keys = jnp.concatenate([prefix_keys, key_part], 0).reshape(-1, HEADS, HEAD_DIM)
    all_values = jnp.concatenate([prefix_values, value_part], 0).reshape(-1, HEADS, HEAD_DIM)
    key_grads = jnp.zeros((PRE + LENGTH, HEADS, HEAD_DIM), jnp.float32)
    value_grads = jnp.zeros((PRE + LENGTH, HEADS, HEAD_DIM), jnp.float32)
    query_grads = []
    for block_index in range(LENGTH // BLOCK):
        start_row = block_index * BLOCK
        limit = start_row + BLOCK
        query_rows = queries[start_row:limit].reshape(BLOCK, HEADS, HEAD_DIM)
        grad_rows = grad_out[start_row:limit].reshape(BLOCK, HEADS, HEAD_DIM)
        keys_here = all_keys[: PRE + limit]
        values_here = all_values[: PRE + limit]
        scores = (
            jnp.einsum("qhd,khd->hqk", query_rows, keys_here, preferred_element_type=jnp.float32)
            * score_scale
        )
        scores = jnp.where(visibility(doc_ids, start_row, limit)[None], scores, masked_score)
        probabilities = jnp.exp(scores - totals[:, start_row:limit][..., None])
        weights_low = probabilities.astype(jnp.bfloat16)
        grad_probs = jnp.einsum(
            "qhd,khd->hqk", grad_rows, values_here, preferred_element_type=jnp.float32
        )
        centre = jnp.sum(probabilities * grad_probs, axis=-1, keepdims=True)
        grad_scores = (probabilities * (grad_probs - centre)).astype(jnp.bfloat16)
        query_grads.append(
            jnp.einsum(
                "hqk,khd->qhd", grad_scores, keys_here, preferred_element_type=jnp.float32
            ).reshape(BLOCK, -1)
            * score_scale
        )
        key_grads = key_grads.at[: PRE + limit].add(
            jnp.einsum("hqk,qhd->khd", grad_scores, query_rows, preferred_element_type=jnp.float32)
            * score_scale
        )
        value_grads = value_grads.at[: PRE + limit].add(
            jnp.einsum("hqk,qhd->khd", weights_low, grad_rows, preferred_element_type=jnp.float32)
        )
    return (
        jnp.concatenate(query_grads, 0),
        key_grads.reshape(PRE + LENGTH, -1),
        value_grads.reshape(PRE + LENGTH, -1),
    )


def layer_forward(hidden, params, prefix_keys, prefix_values, doc_ids):
    (
        attend_gain,
        attend_bias,
        mixing_weight,
        mixing_bias,
        output_weight,
        output_bias,
        feed_gain,
        feed_bias,
        expand_weight,
        expand_bias,
        reduce_weight,
        reduce_bias,
    ) = params
    width = hidden.shape[-1]
    flat_rows = hidden.reshape(-1, width).astype(jnp.float32)
    normed = norm_apply(flat_rows, attend_gain, attend_bias).astype(jnp.bfloat16)
    mixed = (
        jnp.dot(normed, mixing_weight, preferred_element_type=jnp.float32) + mixing_bias
    ).astype(jnp.bfloat16)
    mixed_seq = mixed.reshape(hidden.shape[0], LENGTH, 3 * width)

    def per_sequence(item_pair):
        mixed_one, ids_one = item_pair
        return attend_forward(
            mixed_one[:, :width],
            mixed_one[:, width : 2 * width],
            mixed_one[:, 2 * width :],
            prefix_keys,
            prefix_values,
            ids_one,
        )

    attended, totals = lax.map(per_sequence, (mixed_seq, doc_ids))
    attended_low = attended.reshape(-1, width).astype(jnp.bfloat16)
    middle = (
        flat_rows
        + jnp.dot(attended_low, output_weight, preferred_element_type=jnp.float32)
        + output_bias
    )
    second = norm_apply(middle, feed_gain, feed_bias).astype(jnp.bfloat16)
    expanded = jnp.dot(second, expand_weight, preferred_element_type=jnp.float32) + expand_bias
    activated = gelu_tanh(expanded).astype(jnp.bfloat16)
    result = (
        middle + jnp.dot(activated, reduce_weight, preferred_element_type=jnp.float32) + reduce_bias
    )
    return (result.astype(jnp.bfloat16).reshape(hidden.shape), (mixed, totals, middle, expanded))


def layer_backward(hidden, grad_result, params, prefix_keys, prefix_values, doc_ids, saved):
    (
        attend_gain,
        attend_bias,
        mixing_weight,
        mixing_bias,
        output_weight,
        output_bias,
        feed_gain,
        feed_bias,
        expand_weight,
        expand_bias,
        reduce_weight,
        reduce_bias,
    ) = params
    mixed, totals, middle, expanded = saved
    width = hidden.shape[-1]
    flat_rows = hidden.reshape(-1, width).astype(jnp.float32)
    grad_rows = grad_result.reshape(-1, width)
    grad_activated = contract_last(grad_rows, reduce_weight)
    gelu_pull = jax.vjp(gelu_tanh, expanded)[1]
    grad_expanded = gelu_pull(grad_activated)[0].astype(jnp.bfloat16)
    grad_second = contract_last(grad_expanded, expand_weight)
    feed_pull = jax.vjp(lambda values: norm_apply(values, feed_gain, feed_bias), middle)[1]
    grad_middle = grad_rows.astype(jnp.float32) + feed_pull(grad_second)[0]
    grad_attended = contract_last(grad_middle.astype(jnp.bfloat16), output_weight).astype(
        jnp.bfloat16
    )
    mixed_seq = mixed.reshape(hidden.shape[0], LENGTH, 3 * width)
    grad_seq = grad_attended.reshape(hidden.shape[0], LENGTH, width)

    def per_sequence(item_quad):
        mixed_one, ids_one, totals_one, grad_one = item_quad
        return attend_backward(
            mixed_one[:, :width],
            mixed_one[:, width : 2 * width],
            mixed_one[:, 2 * width :],
            prefix_keys,
            prefix_values,
            ids_one,
            totals_one,
            grad_one,
        )

    query_grads, key_grads, value_grads = lax.map(
        per_sequence, (mixed_seq, doc_ids, totals, grad_seq)
    )
    prefix_grad = jnp.concatenate(
        [jnp.sum(key_grads[:, :PRE], axis=0), jnp.sum(value_grads[:, :PRE], axis=0)], 1
    )
    grad_mixed = jnp.concatenate([query_grads, key_grads[:, PRE:], value_grads[:, PRE:]], -1)
    grad_mixed = grad_mixed.astype(jnp.bfloat16).reshape(-1, 3 * width)
    grad_normed = contract_last(grad_mixed, mixing_weight)
    attend_pull = jax.vjp(lambda values: norm_apply(values, attend_gain, attend_bias), flat_rows)[1]
    grad_hidden = grad_middle + attend_pull(grad_normed)[0]
    return (grad_hidden.astype(jnp.bfloat16).reshape(hidden.shape), prefix_grad)


def place(buffer, item, slot_index, active_slot):
    return jnp.where(
        active_slot, lax.dynamic_update_index_in_dim(buffer, item, slot_index, 0), buffer
    )


def per_device(
    inputs,
    cotangent,
    doc_lengths,
    attend_gain,
    attend_bias,
    mixing_weight,
    mixing_bias,
    output_weight,
    output_bias,
    feed_gain,
    feed_bias,
    expand_weight,
    expand_bias,
    reduce_weight,
    reduce_bias,
    prefix_embed,
    hidden_weight,
    hidden_bias,
    prefix_weight,
    prefix_bias,
):
    section_index = lax.axis_index("section")
    params = tuple(
        (
            entry[0]
            for entry in (
                attend_gain,
                attend_bias,
                mixing_weight,
                mixing_bias,
                output_weight,
                output_bias,
                feed_gain,
                feed_bias,
                expand_weight,
                expand_bias,
                reduce_weight,
                reduce_bias,
            )
        )
    )
    width = inputs.shape[-1]
    seq_count = inputs.shape[1]
    ff_width = expand_weight.shape[-1]
    activity = jnp.tanh(
        jnp.dot(prefix_embed, hidden_weight, preferred_element_type=jnp.float32) + hidden_bias
    )
    activity_low = activity.astype(jnp.bfloat16)
    column_part = (
        jnp.dot(activity_low, prefix_weight[0], preferred_element_type=jnp.float32) + prefix_bias[0]
    ).astype(jnp.bfloat16)
    table = lax.all_gather(column_part, "dp", axis=1, tiled=True)
    prefix_keys = table[:, :width]
    prefix_values = table[:, width:]
    all_ids = document_ids(doc_lengths)
    empty_saved = (
        jnp.zeros((seq_count * LENGTH, 3 * width), jnp.bfloat16),
        jnp.zeros((seq_count, HEADS, LENGTH), jnp.float32),
        jnp.zeros((seq_count * LENGTH, width), jnp.float32),
        jnp.zeros((seq_count * LENGTH, ff_width), jnp.float32),
    )
    saved_start = ()
    carried = (
        jnp.zeros(inputs.shape, jnp.bfloat16),
        jnp.zeros(inputs.shape, jnp.bfloat16),
        saved_start,
    )
    received = jnp.zeros(inputs.shape[1:], jnp.bfloat16)
    for tick_index in range(MICRO + 1):
        micro_index = tick_index - section_index
        active_slot = (micro_index >= 0) & (micro_index < MICRO)
        micro_index = jnp.clip(micro_index, 0, MICRO - 1)
        current = jnp.where(section_index == 0, inputs[min(tick_index, MICRO - 1)], received)
        forward_stored, forward_produced, forward_saved = carried
        forward_doc_ids = lax.dynamic_index_in_dim(all_ids, micro_index, 0, keepdims=False)

        def forward_compute(operands):
            return layer_forward(operands[0], params, prefix_keys, prefix_values, operands[1])

        def forward_skip_slot(operands):
            return (jnp.zeros_like(operands[0]), empty_saved)

        result, extra = lax.cond(
            active_slot, forward_compute, forward_skip_slot, (current, forward_doc_ids)
        )
        forward_stored = place(forward_stored, current, micro_index, active_slot)
        forward_produced = place(forward_produced, result, micro_index, active_slot)
        result, carried = (result, (forward_stored, forward_produced, forward_saved))
        if tick_index < MICRO:
            received = from_behind(result, "section", 1)
    stored, produced, saved = carried

    def backward_slot(grad_in, micro_index, active_slot, state_back):
        gradients_out, prefix_total = state_back
        doc_ids = lax.dynamic_index_in_dim(all_ids, micro_index, 0, keepdims=False)
        hidden = lax.dynamic_index_in_dim(stored, micro_index, 0, keepdims=False)

        def backward_compute(operands):
            extra_now = layer_forward(operands[0], params, prefix_keys, prefix_values, operands[2])[
                1
            ]
            return layer_backward(
                operands[0], operands[1], params, prefix_keys, prefix_values, operands[2], extra_now
            )

        operands = (hidden, grad_in, doc_ids)

        def backward_skip_slot(operands):
            return (jnp.zeros_like(operands[1]), jnp.zeros((PRE, 2 * width), jnp.float32))

        grad_hidden, prefix_grad = lax.cond(
            active_slot, backward_compute, backward_skip_slot, operands
        )
        gradients_out = place(gradients_out, grad_hidden, micro_index, active_slot)
        return (grad_hidden, (gradients_out, prefix_total + prefix_grad))

    state_back = (jnp.zeros(inputs.shape, jnp.bfloat16), jnp.zeros((PRE, 2 * width), jnp.float32))
    received = jnp.zeros(inputs.shape[1:], jnp.bfloat16)
    for tick_index in range(MICRO + 1):
        micro_index = tick_index - 1 + section_index
        active_slot = (micro_index >= 0) & (micro_index < MICRO)
        micro_index = jnp.clip(micro_index, 0, MICRO - 1)
        grad_in = jnp.where(section_index == 1, cotangent[min(tick_index, MICRO - 1)], received)
        grad_hidden, state_back = backward_slot(grad_in, micro_index, active_slot, state_back)
        if tick_index < MICRO:
            received = from_behind(grad_hidden, "section", -1)
    gradients_out, prefix_total = state_back
    exact_mode = lax.Precision.HIGHEST
    prefix_cols = lax.psum_scatter(prefix_total, "dp", scatter_dimension=1, tiled=True)
    grad_prefix_bias = jnp.sum(prefix_cols, axis=0)[None]
    grad_prefix_weight = jnp.dot(
        activity_low.astype(jnp.float32).T, prefix_cols, precision=exact_mode
    )[None]
    activity_part = jnp.dot(
        prefix_cols, prefix_weight[0].astype(jnp.float32).T, precision=exact_mode
    )
    activity_grad = lax.psum(activity_part, ("section", "dp"))
    pre_grad = activity_grad * (1.0 - activity * activity)
    grad_hidden_bias = jnp.sum(pre_grad, axis=0)
    grad_hidden_weight = jnp.dot(prefix_embed.astype(jnp.float32).T, pre_grad, precision=exact_mode)
    grad_embed = jnp.dot(pre_grad, hidden_weight.astype(jnp.float32).T, precision=exact_mode)
    return (
        produced[None],
        gradients_out[None],
        grad_embed,
        grad_hidden_weight,
        grad_hidden_bias,
        grad_prefix_weight,
        grad_prefix_bias,
    )


def solution(mesh):
    in_specs = (
        P(None, "dp", None, None),
        P(None, "dp", None, None),
        P(None, "dp", None),
        P("section", None),
        P("section", None),
        P("section", None, None),
        P("section", None),
        P("section", None, None),
        P("section", None),
        P("section", None),
        P("section", None),
        P("section", None, None),
        P("section", None),
        P("section", None, None),
        P("section", None),
        P(),
        P(),
        P(),
        P("section", None, "dp"),
        P("section", "dp"),
    )
    out_specs = (
        P("section", None, "dp", None, None),
        P("section", None, "dp", None, None),
        P(),
        P(),
        P(),
        P("section", None, "dp"),
        P("section", "dp"),
    )
    return jax.shard_map(
        per_device, mesh=mesh, in_specs=in_specs, out_specs=out_specs, check_vma=False
    )
```

profile of v0, /device:TPU:1, one launch (start us, length us, event | category | flops | bytes accessed | tf_op | source)
XLA Modules:
  0.0 1723.9 jit_solution(722693674115074363)
XLA Ops:
  17.8 34.9 %all_gather.3 = bf16[10,2048]{1,0:T(8,128)(2,1)S(1)} all-gather(bf16[10,128]{1,0:T(8,128)(2,1)S(1)} %fusion.477), channel_id=1, replica_groups=mesh['section'=2,'dp'=16] {'dp'}, dimensions={1}, use_global_device_ids=true | all-gather | bytes 43520 | tf_op jit(solution)/shard_map/all_gather | solution.py:302
  61.3 6.8 conditional.6
  72.3 171.0 %collective-permute-done = bf16[1,1024,1024]{2,1,0:T(8,128)(2,1)} collective-permute-done((bf16[1,1024,1024]{2,1,0:T(8,128)(2,1)S(1)}, bf16[1,1024,1024]{2,1,0:T(8,128)(2,1)}, u32[]{:S(2)}, u32[]{:S(2)}) %collective-permute-start) | collective-permute-done | bytes 2097184 | tf_op jit(solution)/shard_map/ppermute | solution.py:20
  249.8 160.5 %conditional.7 = (bf16[1,1024,1024]{1,2,0:T(8,128)(2,1)}, bf16[1,1,1024,1024]{3,2,1,0:T(8,128)(2,1)}) conditional(s32[]{:T(128)} %convert_element_type.637, () %tuple.200, (bf16[1,1024,1024]{2,1,0:T(8,128)(2,1)}, bf16[1024]{0:T(1024)(128)(2,1)S(1)}, bf16[1024]{0:T(1024)(128)(2,1)S(1)}, bf16[1024,3072]{1,0:T(8,128)(2,1)}, ...), branch_computations={%region_12.13_spmd, %region_13.22_spmd} | conditional | flops 29236281344 | bytes 342778304 | solution.py:333
  259.1 10.3 add_convert_fusion.5
  294.2 10.4 fusion.70
  305.2 9.5 exponential_reduce_fusion.3
  314.7 11.8 fusion.109
  326.5 14.4 fusion.491
  340.9 13.4 exponential_reduce_fusion.2
  354.3 13.7 fusion.108
  375.2 31.3 %add_convert_fusion.6 = bf16[1024,1024]{0,1:T(8,128)(2,1)} fusion(f32[1024,1024]{0,1:T(8,128)} %copy-done.96, bf16[4096,1024]{1,0:T(8,128)(2,1)} %get-tuple-element.1101, f32[4096]{0:T(1024)S(1)} %convert_element_type.538, bf16[1024,4096]{1,0:T(8,128)(2,1)} %get-tuple-element.1099, f32[1024]{0:T(1024)S(1)} %copy-done.191, f32[1024]{0:T(1024)S(1)} %copy-done.195, ...), kind=kOutput, calls=%fused_computation.116 | convolution fusion | flops 17230200832 | bytes 23105536 | tf_op jit(solution)/shard_map/cond/branch_1_fun/dot_general | solution.py:181
  427.3 378.6 %conditional.9 = (bf16[1,1024,1024]{1,2,0:T(8,128)(2,1)}, f32[10,2048]{1,0:T(8,128)}, bf16[1,1,1024,1024]{3,2,1,0:T(8,128)(2,1)}) conditional(s32[]{:T(128)} %convert_element_type.639, () %tuple.204, (bf16[2,1,1024,1024]{3,2,1,0:T(8,128)(2,1)}, pred[1,1024,1024]{1,2,0:T(8,128)(4,1)}, bf16[1,1024,1024]{1,2,0:T(8,128)(2,1)}, ...), branch_computations={%region_32.33_spmd, %region_33.48_spmd} | conditional | flops 53201924096 | bytes 1032398528 | solution.py:361
  451.7 10.3 add_convert_fusion.17
  486.8 17.2 %fusion.517 = f32[1024,4096]{1,0:T(8,128)} fusion(bf16[1024,1024]{0,1:T(8,128)(2,1)} %fusion.230, bf16[4096,1024]{1,0:T(8,128)(2,1)} %get-tuple-element.1123), kind=kOutput, calls=%fused_computation.707 | convolution fusion | flops 8589934592 | bytes 27262976 | tf_op jit(solution)/shard_map/cond/branch_1_fun/dot_general | solution.py:35
  504.1 7.6 fusion.191
  511.7 10.1 exponential_reduce_fusion.7
  522.6 11.7 convolution_convert_fusion
  534.3 14.0 fusion.504
  548.3 13.2 exponential_reduce_fusion.6
  561.5 14.8 fusion.254
  583.5 28.2 %fusion.194.clone.4 = bf16[1024,4096]{1,0:T(8,128)(2,1)} fusion(f32[1024,4096]{1,0:T(8,128)} %fusion.517, f32[4096]{0:T(1024)S(1)} %copy-done.188, bf16[1024,4096]{1,0:T(8,128)(2,1)} %get-tuple-element.1137, f32[1024,1024]{0,1:T(8,128)} %copy-done.43, f32[1024]{0:T(1024)S(1)} %convert_element_type.571, ...), kind=kOutput, calls=%fused_computation.264.clone.clone.clone.clone.1 | convolution fusion | flops 8683257856 | bytes 37781504 | tf_op jit(solution)/shard_map/cond/branch_1_fun/dot_general | solution.py:178
  611.6 14.1 multiply_reduce_fusion.5
  631.8 9.7 convolution_bitcast_fusion
  641.4 16.8 bitcast_add_fusion
  664.6 12.7 multiply_reduce_fusion.4
  677.3 12.6 multiply_convert_fusion.1
  697.0 22.4 %multiply_reduce_fusion.3 = (f32[16,512]{1,0:T(8,128)S(1)}, f32[16,512,1034]{1,2,0:T(8,128)}) fusion(f32[16,512,1034]{1,2,0:T(8,128)} %get-tuple-element.1751, f32[16,512]{1,0:T(8,128)S(1)} %log_add_fusion.6, bf16[512,16,64]{0,2,1:T(8,128)(2,1)S(1)} %bitcast.568, bf16[1034,16,64]{0,2,1:T(8,128)(2,1)S(1)} %bitcast.547), kind=kOutput, calls=%fused_computation.246 | convolution fusion | flops 1109630976 | bytes 70995968 | tf_op jit(solution)/shard_map/cond/branch_1_fun/while/body/eval_jaxpr/qhd,khd->hqk/dot_general | solution.py:111
  719.4 29.0 %multiply_convert_fusion = bf16[16,512,1034]{1,2,0:T(8,128)(2,1)} fusion(f32[16,512,1034]{1,2,0:T(8,128)} %get-tuple-element.1761, f32[16,512,1034]{1,2,0:T(8,128)} %get-tuple-element.1751, f32[16,512]{1,0:T(8,128)S(1)} %get-tuple-element.1760, f32[16,512]{1,0:T(8,128)S(1)} %log_add_fusion.6), kind=kLoop, calls=%fused_computation.245 | loop fusion | flops 33882112 | bytes 84770816 | tf_op jit(solution)/shard_map/cond/branch_1_fun/while/body/eval_jaxpr/convert_element_type | solution.py:115
  748.5 10.0 multiply_convert_fusion.2
  758.4 14.5 bitcast_add_fusion.1
  778.0 11.8 fusion.219
  813.0 373.6 %conditional.10 = (bf16[1,1024,1024]{1,2,0:T(8,128)(2,1)}, f32[10,2048]{1,0:T(8,128)}, bf16[1,1,1024,1024]{3,2,1,0:T(8,128)(2,1)}) conditional(s32[]{:T(128)} %convert_element_type.640, () %tuple.206, (pred[1,1024,1024]{1,2,0:T(8,128)(4,1)}, bf16[1,1024,1024]{1,2,0:T(8,128)(2,1)}, bf16[1,1024,1024]{1,2,0:T(8,128)(2,1)}, ...), branch_computations={%region_48.49_spmd, %region_49.64_spmd} | conditional | flops 53201924096 | bytes 1024009920 | solution.py:361
  832.6 10.3 add_convert_fusion.22
  868.0 17.0 fusion.329
  885.0 7.6 fusion.287
  892.6 10.1 exponential_reduce_fusion.9
  903.5 11.7 convolution_convert_fusion.1
  915.2 14.0 fusion.509
  929.2 13.2 exponential_reduce_fusion.8
  942.4 14.6 fusion.351
  964.1 28.2 %fusion.290.clone.2 = bf16[1024,4096]{1,0:T(8,128)(2,1)} fusion(f32[1024,4096]{1,0:T(8,128)} %fusion.329, f32[4096]{0:T(1024)S(1)} %copy-done.189, bf16[1024,4096]{1,0:T(8,128)(2,1)} %get-tuple-element.1156, f32[1024,1024]{0,1:T(8,128)} %copy-done.45, f32[1024]{0:T(1024)S(1)} %convert_element_type.592, ...), kind=kOutput, calls=%fused_computation.397.clone.clone.clone.clone | convolution fusion | flops 8683257856 | bytes 37781504 | tf_op jit(solution)/shard_map/cond/branch_1_fun/dot_general | solution.py:178
  992.3 14.3 multiply_reduce_fusion.9
  1012.5 9.7 convolution_bitcast_fusion.1
  1022.2 16.8 bitcast_add_fusion.2
  1045.2 12.7 multiply_reduce_fusion.8
  1057.9 12.6 multiply_convert_fusion.5
  1077.7 22.4 %multiply_reduce_fusion.7 = (f32[16,512]{1,0:T(8,128)S(1)}, f32[16,512,1034]{1,2,0:T(8,128)}) fusion(f32[16,512,1034]{1,2,0:T(8,128)} %get-tuple-element.1777, f32[16,512]{1,0:T(8,128)S(1)} %log_add_fusion.8, bf16[512,16,64]{0,2,1:T(8,128)(2,1)S(1)} %bitcast.570, bf16[1034,16,64]{0,2,1:T(8,128)(2,1)S(1)} %bitcast.549), kind=kOutput, calls=%fused_computation.379 | convolution fusion | flops 1109630976 | bytes 70995968 | tf_op jit(solution)/shard_map/cond/branch_1_fun/while/body/eval_jaxpr/qhd,khd->hqk/dot_general | solution.py:111
  1100.1 28.8 %multiply_convert_fusion.4 = bf16[16,512,1034]{1,2,0:T(8,128)(2,1)} fusion(f32[16,512,1034]{1,2,0:T(8,128)} %get-tuple-element.1787, f32[16,512,1034]{1,2,0:T(8,128)} %get-tuple-element.1777, f32[16,512]{1,0:T(8,128)S(1)} %get-tuple-element.1786, f32[16,512]{1,0:T(8,128)S(1)} %log_add_fusion.8), kind=kLoop, calls=%fused_computation.378 | loop fusion | flops 33882112 | bytes 84770816 | tf_op jit(solution)/shard_map/cond/branch_1_fun/while/body/eval_jaxpr/convert_element_type | solution.py:115
  1128.9 10.0 multiply_convert_fusion.6
  1138.9 14.5 bitcast_add_fusion.3
  1158.6 11.8 fusion.315
  1186.5 14.1 collective-permute-start.3
  1208.6 158.7 %conditional.8 = (bf16[1,1,1024,1024]{3,2,1,0:T(8,128)(2,1)}) conditional(s32[]{:T(128)} %convert_element_type.638, () %tuple.202, (bf16[1,1024,1024]{2,1,0:T(8,128)(2,1)}, bf16[1024]{0:T(1024)(128)(2,1)S(1)}, bf16[1024]{0:T(1024)(128)(2,1)S(1)}, bf16[1024,3072]{1,0:T(8,128)(2,1)}, bf16[3072]{0:T(1024)(128)(2,1)S(1)}, ...), branch_computations={%region_22.23_spmd, %region_23.32_spmd} | conditional | flops 29236281344 | bytes 342778272 | solution.py:333
  1218.1 10.3 add_convert_fusion.10
  1253.3 10.4 fusion.130
  1264.3 9.5 exponential_reduce_fusion.5
  1273.8 11.8 fusion.172
  1285.6 14.2 fusion.495
  1299.7 13.4 exponential_reduce_fusion.4
  1313.2 13.7 fusion.171
  1334.0 30.2 %fusion.168 = bf16[1,1,1024,1024]{2,3,1,0:T(8,128)(2,1)S(1)} fusion(f32[1024]{0:T(1024)S(1)} %copy-done.192, f32[1024,1024]{0,1:T(8,128)} %copy-done.97, bf16[4096,1024]{1,0:T(8,128)(2,1)} %get-tuple-element.1118, f32[4096]{0:T(1024)S(1)} %convert_element_type.555, bf16[1024,4096]{1,0:T(8,128)(2,1)} %get-tuple-element.1116, f32[1024]{0:T(1024)S(1)} %copy-done.197, ...), kind=kOutput, calls=%fused_computation.220 | convolution fusion | flops 17230200832 | bytes 23105536 | tf_op jit(solution)/shard_map/cond/branch_1_fun/dot_general | solution.py:181
  1392.6 267.9 %reduce-scatter.2.cloned.1.call-done = f32[10,128]{1,0:T(8,128)} async-done(((f32[10,2048]{1,0:T(8,128)}), f32[10,128]{1,0:T(8,128)}) %reduce-scatter.2.cloned.1.call-update) | async-done | bytes 5136 | tf_op jit(solution)/shard_map/reduce_scatter | solution.py:379
  1661.5 48.7 %psum.7 = f32[10,512]{1,0:T(8,128)S(1)} all-reduce(f32[10,512]{1,0:T(8,128)S(1)} %fusion.478), channel_id=1, replica_groups=mesh['section'=2,'dp'=16] {'section','dp'}, use_global_device_ids=true, to_apply=%region_81.82 | all-reduce | flops 5120 | bytes 40960 | tf_op jit(solution)/shard_map/psum | solution.py:387
  (571 shorter events, 379.8 us)
Async XLA Ops:
  7.2 1653.4 %reduce-scatter.2.cloned.1.call-start = ((), (), s32[]{:S(2)}) async-start(), calls=%async_computation.1 | async-start | bytes 139264 | tf_op jit(solution)/shard_map/reduce_scatter | solution.py:379
  9.7 51.5 %copy-start.130 = (bf16[1024]{0:T(1024)(128)(2,1)}, bf16[1024]{0:T(1024)(128)(2,1)S(1)}, u32[]{:S(2)}) copy-start(bf16[1024]{0:T(1024)(128)(2,1)S(1)} %reduce.37) | copy-start | bytes 6148
  10.4 50.8 %copy-start.136 = (bf16[1024]{0:T(1024)(128)(2,1)}, bf16[1024]{0:T(1024)(128)(2,1)S(1)}, u32[]{:S(2)}) copy-start(bf16[1024]{0:T(1024)(128)(2,1)S(1)} %reduce.38) | copy-start | bytes 6148
  11.1 50.1 %copy-start.142 = (bf16[1024]{0:T(1024)(128)(2,1)}, bf16[1024]{0:T(1024)(128)(2,1)S(1)}, u32[]{:S(2)}) copy-start(bf16[1024]{0:T(1024)(128)(2,1)S(1)} %reduce.40) | copy-start | bytes 6148
  11.8 49.4 %copy-start.148 = (bf16[1024]{0:T(1024)(128)(2,1)}, bf16[1024]{0:T(1024)(128)(2,1)S(1)}, u32[]{:S(2)}) copy-start(bf16[1024]{0:T(1024)(128)(2,1)S(1)} %reduce.41) | copy-start | bytes 6148
  12.6 48.7 %copy-start.154 = (bf16[1024]{0:T(1024)(128)(2,1)}, bf16[1024]{0:T(1024)(128)(2,1)S(1)}, u32[]{:S(2)}) copy-start(bf16[1024]{0:T(1024)(128)(2,1)S(1)} %reduce.42) | copy-start | bytes 6148
  13.3 47.9 %copy-start.185 = (bf16[1024]{0:T(1024)(128)(2,1)}, bf16[1024]{0:T(1024)(128)(2,1)S(1)}, u32[]{:S(2)}) copy-start(bf16[1024]{0:T(1024)(128)(2,1)S(1)} %reduce.44) | copy-start | bytes 6148
  14.2 47.1 %copy-start.115 = (s32[2,1024]{1,0:T(2,128)}, s32[2,1024]{1,0:T(2,128)S(1)}, u32[]{:S(2)}) copy-start(s32[2,1024]{1,0:T(2,128)S(1)} %fusion.481) | copy-start | bytes 24580
  14.9 46.3 %copy-start.121 = (bf16[3072]{0:T(1024)(128)(2,1)}, bf16[3072]{0:T(1024)(128)(2,1)S(1)}, u32[]{:S(2)}) copy-start(bf16[3072]{0:T(1024)(128)(2,1)S(1)} %reduce.39) | copy-start | bytes 18436
  15.7 45.5 %copy-start.109 = (bf16[4096]{0:T(1024)(128)(2,1)}, bf16[4096]{0:T(1024)(128)(2,1)S(1)}, u32[]{:S(2)}) copy-start(bf16[4096]{0:T(1024)(128)(2,1)S(1)} %reduce.43) | copy-start | bytes 24580
  70.9 172.3 %collective-permute-start = (bf16[1,1024,1024]{2,1,0:T(8,128)(2,1)S(1)}, bf16[1,1024,1024]{2,1,0:T(8,128)(2,1)}, u32[]{:S(2)}, u32[]{:S(2)}) collective-permute-start(bf16[1,1024,1024]{2,1,0:T(8,128)(2,1)S(1)} %copy.280), channel_id=1, source_target_pairs={{0,16},{1,17},{2,18},{3,19},{4,20},{5,21},{6,22},{7,23},{8,24},{9,... | collective-permute-start | bytes 6291464 | tf_op jit(solution)/shard_map/ppermute | solution.py:20
  314.7 11.8 copy-start.63
  314.7 11.8 copy-start.80
  340.9 13.4 copy-start.60
  354.3 13.7 copy-start.25
  354.3 13.7 copy-start.200
  413.2 6.2 collective-permute-start.1
  427.4 24.2 %copy-start.173 = (f32[1024]{0:T(1024)}, f32[1024]{0:T(1024)S(1)}, u32[]{:S(2)}) copy-start(f32[1024]{0:T(1024)S(1)} %convert_element_type.562) | copy-start | bytes 12292 | tf_op jit(solution)/shard_map/cond
  439.0 12.7 copy-start.161
  486.8 47.5 %copy-start.3 = (bf16[1034,1024]{0,1:T(8,128)(2,1)}, bf16[1034,1024]{0,1:T(8,128)(2,1)S(1)}, u32[]{:S(2)}) copy-start(bf16[1034,1024]{0,1:T(8,128)(2,1)S(1)} %copy.257) | copy-start | bytes 6352900 | tf_op jit(solution)/shard_map/cond
  486.8 17.3 %copy-start.34 = (bf16[522,1024]{0,1:T(8,128)(2,1)S(1)}, bf16[522,1024]{0,1:T(8,128)(2,1)}, u32[]{:S(2)}) copy-start(bf16[522,1024]{0,1:T(8,128)(2,1)} %copy.254) | copy-start | bytes 3207172 | tf_op jit(solution)/shard_map/cond
  486.8 17.3 %copy-start.52 = (bf16[512,1024]{0,1:T(8,128)(2,1)S(1)}, bf16[512,1024]{0,1:T(8,128)(2,1)}, u32[]{:S(2)}) copy-start(bf16[512,1024]{0,1:T(8,128)(2,1)} %copy.253) | copy-start | bytes 3145732 | tf_op jit(solution)/shard_map/cond
  486.8 17.3 %copy-start.73 = (pred[512,522]{0,1:T(8,128)(4,1)S(1)}, pred[512,522]{0,1:T(8,128)(4,1)}, u32[]{:S(2)}) copy-start(pred[512,522]{0,1:T(8,128)(4,1)} %concatenate.259) | copy-start | bytes 801796 | tf_op jit(solution)/shard_map/cond
  522.5 11.7 copy-start.49
  522.5 11.7 copy-start.82
  561.5 14.9 copy-start.8
  583.5 28.2 %copy-start.44 = (f32[1024,1024]{0,1:T(8,128)S(1)}, f32[1024,1024]{0,1:T(8,128)}, u32[]{:S(2)}) copy-start(f32[1024,1024]{0,1:T(8,128)} %copy-done.43) | copy-start | bytes 12582916 | tf_op jit(solution)/shard_map/cond
  677.3 12.6 copy-start.35
  719.4 29.0 %copy-start.4 = (bf16[1034,1024]{0,1:T(8,128)(2,1)S(1)}, bf16[1034,1024]{0,1:T(8,128)(2,1)}, u32[]{:S(2)}) copy-start(bf16[1034,1024]{0,1:T(8,128)(2,1)} %copy-done.3) | copy-start | bytes 6352900 | tf_op jit(solution)/shard_map/cond
  758.4 19.5 %copy-start.103 = (bf16[1024,1024]{0,1:T(8,128)(2,1)S(1)}, bf16[1024,1024]{0,1:T(8,128)(2,1)}, u32[]{:S(2)}) copy-start(bf16[1024,1024]{0,1:T(8,128)(2,1)} %fusion.227) | copy-start | bytes 6291460 | tf_op jit(solution)/shard_map/cond
  758.4 19.5 %copy-start.162 = (f32[1024]{0:T(1024)S(1)}, f32[1024]{0:T(1024)}, u32[]{:S(2)}) copy-start(f32[1024]{0:T(1024)} %copy-done.161) | copy-start | bytes 12292 | tf_op jit(solution)/shard_map/cond
  758.4 19.6 %copy-start.174 = (f32[1024]{0:T(1024)S(1)}, f32[1024]{0:T(1024)}, u32[]{:S(2)}) copy-start(f32[1024]{0:T(1024)} %copy-done.173) | copy-start | bytes 12292 | tf_op jit(solution)/shard_map/cond
  778.0 13.2 copy-start.168
  778.0 13.2 copy-start.127
  778.0 13.9 copy-start.180
  805.9 7.0 collective-permute-start.2
  813.1 19.5 %copy-start.175 = (f32[1024]{0:T(1024)}, f32[1024]{0:T(1024)S(1)}, u32[]{:S(2)}) copy-start(f32[1024]{0:T(1024)S(1)} %convert_element_type.583) | copy-start | bytes 12292 | tf_op jit(solution)/shard_map/cond
  829.8 13.2 copy-start.163
  868.0 47.2 %copy-start.5 = (bf16[1034,1024]{0,1:T(8,128)(2,1)}, bf16[1034,1024]{0,1:T(8,128)(2,1)S(1)}, u32[]{:S(2)}) copy-start(bf16[1034,1024]{0,1:T(8,128)(2,1)S(1)} %copy.265) | copy-start | bytes 6352900 | tf_op jit(solution)/shard_map/cond
  868.0 17.0 copy-start.36
  868.0 17.0 copy-start.54
  868.0 17.0 copy-start.75
  903.4 11.7 copy-start.50
  903.5 11.7 copy-start.83
  942.4 14.6 copy-start.12
  964.1 28.2 %copy-start.46 = (f32[1024,1024]{0,1:T(8,128)S(1)}, f32[1024,1024]{0,1:T(8,128)}, u32[]{:S(2)}) copy-start(f32[1024,1024]{0,1:T(8,128)} %copy-done.45) | copy-start | bytes 12582916 | tf_op jit(solution)/shard_map/cond
  1057.9 12.6 copy-start.37
  1100.1 28.8 %copy-start.6 = (bf16[1034,1024]{0,1:T(8,128)(2,1)S(1)}, bf16[1034,1024]{0,1:T(8,128)(2,1)}, u32[]{:S(2)}) copy-start(bf16[1034,1024]{0,1:T(8,128)(2,1)} %copy-done.5) | copy-start | bytes 6352900 | tf_op jit(solution)/shard_map/cond
  1138.9 19.5 %copy-start.104 = (bf16[1024,1024]{0,1:T(8,128)(2,1)S(1)}, bf16[1024,1024]{0,1:T(8,128)(2,1)}, u32[]{:S(2)}) copy-start(bf16[1024,1024]{0,1:T(8,128)(2,1)} %fusion.323) | copy-start | bytes 6291460 | tf_op jit(solution)/shard_map/cond
  1138.9 19.6 %copy-start.164 = (f32[1024]{0:T(1024)S(1)}, f32[1024]{0:T(1024)}, u32[]{:S(2)}) copy-start(f32[1024]{0:T(1024)} %copy-done.163) | copy-start | bytes 12292 | tf_op jit(solution)/shard_map/cond
  1138.9 19.6 %copy-start.176 = (f32[1024]{0:T(1024)S(1)}, f32[1024]{0:T(1024)}, u32[]{:S(2)}) copy-start(f32[1024]{0:T(1024)} %copy-done.175) | copy-start | bytes 12292 | tf_op jit(solution)/shard_map/cond
  1158.5 13.2 copy-start.170
  1158.5 13.2 copy-start.128
  1158.6 13.9 copy-start.182
  1186.5 194.7 %collective-permute-start.3 = (bf16[1,1024,1024]{1,2,0:T(8,128)(2,1)}, bf16[1,1024,1024]{1,2,0:T(8,128)(2,1)}, u32[]{:S(2)}, u32[]{:S(2)}) collective-permute-start(bf16[1,1024,1024]{1,2,0:T(8,128)(2,1)} %get-tuple-element.1203), channel_id=1, source_target_pairs={{16,0},{17,1},{18,2},{19,3},{20,4},{21,5},{22,6},{23,7},{24,8},{25... | collective-permute-start | bytes 6291464 | tf_op jit(solution)/shard_map/ppermute | solution.py:20
  1273.8 11.8 copy-start.64
  1273.8 11.8 copy-start.81
  1299.7 13.4 copy-start.61
  1313.2 13.7 copy-start.27
  1313.2 13.7 copy-start.201
  1386.9 273.6 %copy-start.108 = (bf16[1,512,128]{2,1,0:T(8,128)(2,1)S(1)}, bf16[1,512,128]{2,1,0:T(8,128)(2,1)}, u32[]{:S(2)}) copy-start(bf16[1,512,128]{2,1,0:T(8,128)(2,1)} %param.86) | copy-start | bytes 393220
  1387.0 323.2 %copy-start.107 = (f32[10,512]{1,0:T(8,128)S(1)}, f32[10,512]{1,0:T(8,128)}, u32[]{:S(2)}) copy-start(f32[10,512]{1,0:T(8,128)} %copy-done.106) | copy-start | bytes 61444
  1387.0 325.4 %copy-start.129 = (bf16[10,1024]{1,0:T(8,128)(2,1)S(1)}, bf16[10,1024]{1,0:T(8,128)(2,1)}, u32[]{:S(2)}) copy-start(bf16[10,1024]{1,0:T(8,128)(2,1)} %param.83) | copy-start | bytes 61444
  1660.6 54.7 %copy-start.160 = (f32[10,128]{1,0:T(8,128)S(1)}, f32[10,128]{1,0:T(8,128)}, u32[]{:S(2)}) copy-start(f32[10,128]{1,0:T(8,128)} %reduce-scatter.2.cloned.1.call-done) | copy-start | bytes 15364
  (101 other events, 450.3 us)
Sparse Core Ops, SparseCore 0:
  1388.9 271.6 reduce-scatter.1
where the time goes:
time: 1730 us; the launch traced here: 1720 us
  matrix products  657 us (38%)
  waiting for transfers between devices  443 us (26%)
  other arithmetic  304 us (18%)
  local copies, waits for them, and re-layouts  191 us (11%)
  blocking collectives  83.5 us (5%)
  starting transfers between devices  19.7 us (1%)
    reduce_scatter x1, waiting for transfers between devices, per_device(): lax.psum_scatter(prefix_total, 'dp', scatter_dimension=1, tiled=True)  268 us
    ppermute x4, waiting for transfers between devices, from_behind(): return lax.ppermute(block, axis, route)  175 us
    dot_general x8, matrix products, attend_forward(): jnp.einsum('hqk,khd->qhd', weights_low, all_values[:PRE + limit], preferr...  104 us
    dot_general x8, matrix products, attend_forward(): jnp.einsum('qhd,khd->hqk', query_rows, all_keys[:PRE + limit], preferred_...  92.5 us
    reduce_sum x8, other arithmetic, attend_forward(): log_total = jax.nn.logsumexp(scores, axis=-1)  92.3 us
    dot_general x8, matrix products, contract_last(): lax.dot_general(left, right, (((1,), (1,)), ((), ())), preferred_element_...  91 us
    convert_element_type x4, other arithmetic, attend_backward(): grad_scores = (probabilities * (grad_probs - centre)).astype(jnp.bfloat16)  83 us
    dot_general x4, matrix products, attend_backward(): jnp.einsum('qhd,khd->hqk', grad_rows, values_here, preferred_element_type...  70.2 us
  transfers between devices with their start and end apart: 5, of which 3 were waited for; matrix products, arithmetic and copies ran while one was open for 11% of the time, Pallas kernels for 0%

commit v1 on v0

v1 whole, which is shorter than its diff:
```python
import jax
import jax.numpy as jnp
from jax import lax
from jax.experimental import pallas as pl
from jax.experimental.pallas import tpu as pltpu
from jax.sharding import PartitionSpec as P

F32 = jnp.float32
BF = jnp.bfloat16
LENGTH = 1024
WIDTH = 1024
FF = 4096
HEADS = 16
PRE = 10
PAD = 16
DOCS = 8
QB = 128
KC = 128
PAIRS = 8
STEPS = 5
NEG = -1e9
C0 = 0.7978845608028654
C1 = C0 * 0.044715

ANY = pl.BlockSpec(memory_space=pl.ANY)
SMEM = pl.BlockSpec(memory_space=pltpu.SMEM)
VMEM = pl.BlockSpec(memory_space=pltpu.VMEM)


def dot(a, b):
    return jnp.dot(a, b, preferred_element_type=F32)


def dot_nt(a, b):
    return lax.dot_general(a, b, (((1,), (1,)), ((), ())), preferred_element_type=F32)


def dot_tn(a, b):
    return lax.dot_general(a, b, (((0,), (0,)), ((), ())), preferred_element_type=F32)


def split(value):
    high = value.astype(BF)
    return high, (value - high.astype(F32)).astype(BF)


def call(kernel, ins, in_specs, outs, scratch, name, flops=0, moved=0, out_specs=None):
    return pl.pallas_call(
        kernel,
        in_specs=in_specs,
        out_specs=out_specs or [ANY] * len(outs),
        out_shape=[jax.ShapeDtypeStruct(s, d) for s, d in outs],
        scratch_shapes=scratch,
        compiler_params=pltpu.CompilerParams(vmem_limit_bytes=60 << 20),
        cost_estimate=pl.CostEstimate(flops=flops, bytes_accessed=moved, transcendentals=0),
        name=name,
    )(*ins)


class Copy:
    def __init__(self, source, target, sem, other=None, own=None):
        self.first = pltpu.make_async_copy(source, target, sem)
        self.second = None if other is None else pltpu.make_async_copy(other, target, sem)
        self.own = own

    def start(self):
        if self.second is None:
            self.first.start()
        else:
            pl.when(self.own)(self.first.start)
            pl.when(jnp.logical_not(self.own))(self.second.start)
        return self

    def wait(self):
        self.first.wait()


class Sems:
    def __init__(self, ref):
        self.ref = ref
        self.used = 0

    def __call__(self):
        self.used += 1
        return self.ref.at[self.used - 1]


GAIN_A, BIAS_A, BIAS_M, BIAS_O, GAIN_F, BIAS_F, BIAS_E, BIAS_R = 0, 1, 2, 5, 6, 7, 8, 12


def tile(index, rows):
    return slice(index * rows, (index + 1) * rows)


def normalise(values):
    centre = jnp.mean(values, axis=-1, keepdims=True)
    shifted = values - centre
    variance = jnp.mean(shifted * shifted, axis=-1, keepdims=True)
    scale = lax.rsqrt(variance + 1e-5)
    return shifted * scale, scale


def norm_back(grad, gain, hat, scale):
    weighted = grad * gain
    first = jnp.mean(weighted, axis=-1, keepdims=True)
    second = jnp.mean(weighted * hat, axis=-1, keepdims=True)
    return scale * (weighted - first - hat * second)


def document_ends(lens, row):
    ends, total = [], None
    for doc in range(DOCS - 1):
        total = lens[row, doc] if total is None else total + lens[row, doc]
        ends.append(total)
    return ends


def window(ends, block):
    first = block * QB
    low = jnp.int32(0)
    for end in ends:
        low = jnp.maximum(low, jnp.where(first >= end, end, 0))
    count = (first + QB - low + KC - 1) // KC
    start = jnp.maximum(first + QB - count * KC, 0)
    return first, count, start


def visible(ends, first, start, count):
    places = first + lax.broadcasted_iota(jnp.int32, (1, QB), 1)
    low = jnp.zeros((1, QB), jnp.int32)
    for end in ends:
        low = jnp.maximum(low, jnp.where(places >= end, end, 0))
    keys = start + lax.broadcasted_iota(jnp.int32, (count * KC, QB), 0)
    inside = jnp.where((keys <= places) & (keys >= low), 0.0, NEG).astype(F32)
    prefix = lax.broadcasted_iota(jnp.int32, (PAD, QB), 0)
    prefix = jnp.where(prefix < PRE, 0.0, NEG).astype(F32)
    mask = jnp.concatenate([prefix, inside], 0)
    return jnp.concatenate([mask, mask], 1)


def spread(block):
    lane = lax.broadcasted_iota(jnp.int32, block.shape, 1) // 64
    zero = jnp.zeros_like(block)
    return jnp.concatenate([jnp.where(lane == h, block, zero) for h in range(2)], 0)


def gather_heads(block):
    both = [block[h * 64 : h * 64 + 64, h * QB : h * QB + QB] for h in range(2)]
    return jnp.concatenate(both, 0).T


def columns(pair, third):
    return slice(third * WIDTH + pair * 128, third * WIDTH + pair * 128 + 128)


def attend_step(refs, ends, first, start, count, block):
    mixed, table, attended, totals = refs
    mask = visible(ends, first, start, count)
    rows = pl.ds(pl.multiple_of(first, QB), QB)
    keys = pl.ds(pl.multiple_of(start, QB), count * KC)
    lanes = pl.ds(pl.multiple_of(first, QB), QB)
    pairs = range(PAIRS)
    scores = [
        dot_nt(
            jnp.concatenate([table[:, columns(p, 0)], mixed[keys, columns(p, 1)]], 0),
            spread(mixed[rows, columns(p, 0)]),
        )
        + mask
        for p in pairs
    ]
    tops = [jnp.max(s, 0, keepdims=True) for s in scores]
    raised = [jnp.exp(s - t) for s, t in zip(scores, tops)]
    sums = [jnp.sum(r, 0, keepdims=True) for r in raised]
    low = [r.astype(BF) for r in raised]
    outs = [
        dot_tn(
            jnp.concatenate([table[:, columns(p, 1)], mixed[keys, columns(p, 2)]], 0), low[p]
        )
        for p in pairs
    ]
    for p in pairs:
        log_total = tops[p] + jnp.log(sums[p])
        for h in range(2):
            totals[pl.ds(2 * p + h, 1), lanes] = log_total[:, h * QB : h * QB + QB]
        attended[rows, columns(p, 0)] = gather_heads(outs[p] * (1.0 / sums[p])).astype(BF)


def attend(mixed, table, lens, row, attended, totals):
    ends = document_ends(lens, row)

    def step(block, carry):
        first, count, start = window(ends, block)
        for size in range(1, STEPS + 1):

            @pl.when(count == size)
            def _():
                attend_step((mixed, table, attended, totals), ends, first, start, size, block)

        return carry

    lax.fori_loop(0, LENGTH // QB, step, 0)


def attend_back_step(refs, ends, first, start, count, block):
    mixed, grad_out, totals, centres, table, grad_mixed, key_sum, value_sum = refs
    mask = visible(ends, first, start, count)
    rows = pl.ds(pl.multiple_of(first, QB), QB)
    keys = pl.ds(pl.multiple_of(start, QB), count * KC)
    lanes = pl.ds(pl.multiple_of(first, QB), QB)
    pairs = range(PAIRS)

    def row_of(ref, p):
        return jnp.concatenate([ref[pl.ds(2 * p + h, 1), lanes] for h in range(2)], 1)

    queries = [spread(mixed[rows, columns(p, 0)]) for p in pairs]
    grads = [spread(grad_out[rows, columns(p, 0)]) for p in pairs]
    all_keys = [
        jnp.concatenate([table[:, columns(p, 0)], mixed[keys, columns(p, 1)]], 0) for p in pairs
    ]
    all_values = [
        jnp.concatenate([table[:, columns(p, 1)], mixed[keys, columns(p, 2)]], 0) for p in pairs
    ]
    scores = [dot_nt(all_keys[p], queries[p]) for p in pairs]
    grad_probs = [dot_nt(all_values[p], grads[p]) for p in pairs]
    probs = [jnp.exp(scores[p] + (mask - row_of(totals, p))) for p in pairs]
    low = [p.astype(BF) for p in probs]
    value_grads = [dot(low[p][PAD:], grads[p]) for p in pairs]
    grad_scores = [(probs[p] * (grad_probs[p] - row_of(centres, p))).astype(BF) for p in pairs]
    key_grads = [dot(grad_scores[p][PAD:], queries[p]) for p in pairs]
    query_grads = [dot_tn(all_keys[p], grad_scores[p]) for p in pairs]
    for p in pairs:
        grad_mixed[rows, columns(p, 0)] = (gather_heads(query_grads[p]) * 0.125).astype(BF)
        value_sum[keys, columns(p, 0)] += value_grads[p]
        key_sum[keys, columns(p, 0)] += key_grads[p]


def attend_back(mixed, grad_out, totals, centres, table, lens, row, grad_mixed, sums):
    ends = document_ends(lens, row)
    key_sum, value_sum = sums

    def clear(index, carry):
        rows = pl.ds(pl.multiple_of(index * 64, 64), 64)
        key_sum[rows, :] = jnp.zeros((64, WIDTH), F32)
        value_sum[rows, :] = jnp.zeros((64, WIDTH), F32)
        return carry

    lax.fori_loop(0, LENGTH // 64, clear, 0)

    def step(block, carry):
        first, count, start = window(ends, block)
        for size in range(1, STEPS + 1):

            @pl.when(count == size)
            def _():
                refs = (mixed, grad_out, totals, centres, table, grad_mixed, key_sum, value_sum)
                attend_back_step(refs, ends, first, start, size, block)

        return carry

    lax.fori_loop(0, LENGTH // QB, step, 0)

    def finish(index, carry):
        rows = pl.ds(pl.multiple_of(index * 64, 64), 64)
        grad_mixed[rows, WIDTH : 2 * WIDTH] = key_sum[rows, :].astype(BF)
        grad_mixed[rows, 2 * WIDTH :] = value_sum[rows, :].astype(BF)
        return carry

    lax.fori_loop(0, LENGTH // 64, finish, 0)


def prefix_back(queries, grad_out, attended, totals, centres, table, grad_table):
    heads = lax.broadcasted_iota(jnp.int32, (HEADS, WIDTH), 0)
    lanes = lax.broadcasted_iota(jnp.int32, (HEADS, WIDTH), 1)
    pick = jnp.where(lanes // 64 == heads, 1.0, 0.0).astype(BF)
    high, low = split(attended[...].astype(F32) * grad_out[...].astype(F32))
    centre = dot_nt(pick, high) + dot_nt(pick, low)
    centres[...] = centre
    real = lax.broadcasted_iota(jnp.int32, (4 * PAD, LENGTH), 0) % PAD < PRE
    lane = lax.broadcasted_iota(jnp.int32, (PAD, 256), 1) // 64

    def widen(block):
        zero = jnp.zeros_like(block)
        return jnp.concatenate([jnp.where(lane == h, block, zero) for h in range(4)], 0)

    def narrow(block):
        result = block[:PAD]
        for h in range(1, 4):
            result = jnp.where(lane == h, block[h * PAD : (h + 1) * PAD], result)
        return result

    def repeat(rows):
        return jnp.concatenate(
            [jnp.broadcast_to(rows[h : h + 1], (PAD, LENGTH)) for h in range(4)], 0
        )

    for quad in range(4):
        cols = slice(quad * 256, quad * 256 + 256)
        later = slice(WIDTH + quad * 256, WIDTH + quad * 256 + 256)
        mine = slice(quad * 4, quad * 4 + 4)
        scores = dot_nt(widen(table[:, cols]), queries[:, cols]) - repeat(totals[mine, :])
        probs = jnp.where(real, jnp.exp(scores), 0.0)
        grad_probs = dot_nt(widen(table[:, later]), grad_out[:, cols])
        grad_scores = (probs * (grad_probs - repeat(centre[mine, :]))).astype(BF)
        grad_table[:, cols] = narrow(dot(grad_scores, queries[:, cols]))
        grad_table[:, later] = narrow(dot(probs.astype(BF), grad_out[:, cols]))


def vm(shape, dtype=BF):
    return pltpu.VMEM(shape, dtype)


DMA = pltpu.SemaphoreType.DMA


def mix_kernel(layer):
    def kernel(sec, x, pack, pack2, w, w2, mixed, x_v, n_v, w_v, p_v, m_v, sems):
        own = sec[0] == layer
        sem = Sems(sems)
        source = x.at[sec[0]] if layer == 0 else x
        packs = Copy(pack, p_v, sem(), pack2, own).start()
        xs = [Copy(source.at[tile(r, 256)], x_v.at[tile(r, 256)], sem()).start() for r in range(4)]
        ws = [
            Copy(
                w.at[:, tile(j, WIDTH)], w_v.at[:, tile(j, WIDTH)], sem(),
                w2.at[:, tile(j, WIDTH)], own,
            ).start()
            for j in range(3)
        ]
        packs.wait()
        gain, bias = p_v[GAIN_A : GAIN_A + 1], p_v[BIAS_A : BIAS_A + 1]

        def norm(r):
            xs[r].wait()
            hat, _ = normalise(x_v[tile(r, 256)].astype(F32))
            n_v[tile(r, 256)] = (hat * gain + bias).astype(BF)

        norm(0)
        outs = []
        for j in range(3):
            ws[j].wait()
            cols = tile(j, WIDTH)
            for r in range(4):
                value = dot(n_v[tile(r, 256)], w_v[:, cols]) + p_v[BIAS_M + j : BIAS_M + j + 1]
                value = value.astype(BF)
                if j == 0:
                    value = value * jnp.asarray(0.125, BF)
                    if r < 3:
                        norm(r + 1)
                m_v[tile(r, 256), cols] = value
            outs.append(Copy(m_v.at[:, cols], mixed.at[:, cols], sem()).start())
        for out in outs:
            out.wait()

    return kernel


def mix(layer, sec, x, packs, weights):
    return call(
        mix_kernel(layer),
        (sec, x, *packs, *weights),
        [SMEM] + [ANY] * 5,
        [((LENGTH, 3 * WIDTH), BF)],
        [
            vm((LENGTH, WIDTH)), vm((LENGTH, WIDTH)), vm((WIDTH, 3 * WIDTH)), vm((16, 1024), F32),
            vm((LENGTH, 3 * WIDTH)), DMA((16,)),
        ],
        f"mix{layer}", 2 * LENGTH * WIDTH * 3 * WIDTH, 14 << 20,
    )[0]


def gelu_both(value):
    square = value * value
    half = 0.5 * jnp.tanh(value * (C1 * square + C0)) + 0.5
    result = value * half
    return result, half + result * (1.0 - half) * ((6 * C1) * square + 2 * C0)


def attend_kernel(layer):
    def kernel(
        sec, lens, x, mixed, table, pack, pack2, wo, wo2, we, we2,
        attended, totals, middle, slope, active,
        x_v, m_v, t_v, p_v, wo_v, we_v, at_v, to_v, mid_v, s_v, a_v, sems,
    ):
        own = sec[0] == layer
        sem = Sems(sems)
        source = x.at[sec[0]] if layer == 0 else x
        first = [Copy(mixed, m_v, sem()).start(), Copy(table, t_v, sem()).start()]
        packs = Copy(pack, p_v, sem(), pack2, own).start()
        later = [Copy(source, x_v, sem()).start(), Copy(wo, wo_v, sem(), wo2, own).start()]
        wes = [
            Copy(
                we.at[:, tile(j, 1024)], we_v.at[:, tile(j, 1024)], sem(),
                we2.at[:, tile(j, 1024)], own,
            ).start()
            for j in range(4)
        ]
        for copy in first:
            copy.wait()
        attend(m_v, t_v, lens, sec[0], at_v, to_v)
        outs = [Copy(at_v, attended, sem()).start(), Copy(to_v, totals, sem()).start()]
        for copy in later:
            copy.wait()
        packs.wait()
        gain, bias = p_v[GAIN_F : GAIN_F + 1], p_v[BIAS_F : BIAS_F + 1]
        seconds = []
        for r in range(4):
            rows = tile(r, 256)
            value = x_v[rows].astype(F32) + dot(at_v[rows], wo_v[...]) + p_v[BIAS_O : BIAS_O + 1]
            mid_v[rows] = value
            hat, _ = normalise(value)
            x_v[rows] = (hat * gain + bias).astype(BF)
        outs.append(Copy(mid_v, middle, sem()).start())
        for j in range(4):
            wes[j].wait()
        for r in range(2):
            rows = tile(r, 512)
            for j in range(8):
                cols = tile(j, 512)
                part = slice((j % 2) * 512, (j % 2) * 512 + 512)
                row = BIAS_E + j // 2
                value = dot(x_v[rows], we_v[:, cols]) + p_v[row : row + 1, part]
                result, derivative = gelu_both(value)
                a_v[rows, cols] = result.astype(BF)
                s_v[rows, cols] = derivative.astype(BF)
            outs.append(Copy(a_v.at[rows], active.at[rows], sem()).start())
            outs.append(Copy(s_v.at[rows], slope.at[rows], sem()).start())
        for out in outs:
            out.wait()

    return kernel


def attend_expand(layer, sec, lens, x, mixed, table, packs, wo, we):
    return call(
        attend_kernel(layer),
        (sec, lens, x, mixed, table, *packs, *wo, *we),
        [SMEM, SMEM] + [ANY] * 9,
        [
            ((LENGTH, WIDTH), BF), ((HEADS, LENGTH), F32), ((LENGTH, WIDTH), F32),
            ((LENGTH, FF), BF), ((LENGTH, FF), BF),
        ],
        [
            vm((LENGTH, WIDTH)), vm((LENGTH, 3 * WIDTH)), vm((PAD, 2 * WIDTH)), vm((16, 1024), F32),
            vm((WIDTH, WIDTH)), vm((WIDTH, FF)), vm((LENGTH, WIDTH)), vm((HEADS, LENGTH), F32),
            vm((LENGTH, WIDTH), F32), vm((LENGTH, FF)), vm((LENGTH, FF)), DMA((20,)),
        ],
        f"attend_expand{layer}", 2 * LENGTH * WIDTH * 8 * WIDTH, 44 << 20,
    )


def reduce_kernel(layer):
    def kernel(sec, active, middle, pack, pack2, wr, wr2, out, a_v, mid_v, p_v, w_v, o_v, sems):
        own = sec[0] == layer
        sem = Sems(sems)
        packs = Copy(pack, p_v, sem(), pack2, own).start()
        acts = [Copy(active.at[tile(0, 256)], a_v.at[tile(0, 256)], sem()).start()]
        mids = [Copy(middle, mid_v, sem())]
        ws = [
            Copy(
                wr.at[:, tile(n, 256)], w_v.at[:, tile(n, 256)], sem(),
                wr2.at[:, tile(n, 256)], own,
            ).start()
            for n in range(4)
        ]
        mids[0].start()
        for r in range(1, 4):
            acts.append(Copy(active.at[tile(r, 256)], a_v.at[tile(r, 256)], sem()).start())
        packs.wait()
        outs = []
        for r in range(4):
            rows = tile(r, 256)
            acts[r].wait()
            for n in range(4):
                cols = tile(n, 256)
                if r == 0:
                    ws[n].wait()
                value = dot(a_v[rows], w_v[:, cols]) + p_v[BIAS_R : BIAS_R + 1, cols]
                if r == 0 and n == 0:
                    mids[0].wait()
                o_v[rows, cols] = (mid_v[rows, cols] + value).astype(BF)
            outs.append(Copy(o_v.at[rows], out.at[rows], sem()).start())
        for copy in outs:
            copy.wait()

    return kernel


def reduce(layer, sec, active, middle, packs, wr):
    return call(
        reduce_kernel(layer),
        (sec, active, middle, *packs, *wr),
        [SMEM] + [ANY] * 6,
        [((LENGTH, WIDTH), BF)],
        [
            vm((LENGTH, FF)), vm((LENGTH, WIDTH), F32), vm((16, 1024), F32), vm((FF, WIDTH)),
            vm((LENGTH, WIDTH)), DMA((16,)),
        ],
        f"reduce{layer}", 2 * LENGTH * WIDTH * FF, 22 << 20,
    )[0]


def feed_back_kernel(layer):
    def kernel(
        sec, g, slope, middle, mixed, attended, totals, table, pack, pack2, wo, wo2, we, we2, wr, wr2,
        grad_middle, grad_out, centres, grad_table,
        g_v, s_v, mid_v, q_v, at_v, to_v, t_v, p_v, wo_v, we_v, wr_v, acc_v, go_v, c_v, gt_v, sems,
    ):
        own = sec[0] == layer
        sem = Sems(sems)
        source = g.at[sec[0]] if layer == 1 else g
        gs = Copy(source, g_v, sem()).start()
        parts = []
        for c in range(8):
            cols = tile(c, 512)
            parts.append([
                Copy(wr.at[cols], wr_v.at[cols], sem(), wr2.at[cols], own).start(),
                Copy(slope.at[:, cols], s_v.at[:, cols], sem()).start(),
                Copy(we.at[:, cols], we_v.at[:, cols], sem(), we2.at[:, cols], own).start(),
            ])
        packs = Copy(pack, p_v, sem(), pack2, own).start()
        mids = Copy(middle, mid_v, sem()).start()
        wos = Copy(wo, wo_v, sem(), wo2, own).start()
        later = [
            Copy(mixed.at[:, :WIDTH], q_v, sem()).start(),
            Copy(attended, at_v, sem()).start(),
            Copy(totals, to_v, sem()).start(),
            Copy(table, t_v, sem()).start(),
        ]
        gs.wait()
        for r in range(2):
            rows = tile(r, 512)
            total = None
            for c in range(8):
                cols = tile(c, 512)
                if r == 0:
                    for copy in parts[c]:
                        copy.wait()
                value = dot_nt(g_v[rows], wr_v[cols]) * s_v[rows, cols].astype(F32)
                value = dot_nt(value.astype(BF), we_v[:, cols])
                total = value if total is None else total + value
            acc_v[rows] = total
        packs.wait()
        mids.wait()
        wos.wait()
        gain = p_v[GAIN_F : GAIN_F + 1]
        outs = []
        for r in range(4):
            rows = tile(r, 256)
            hat, scale = normalise(mid_v[rows])
            value = g_v[rows].astype(F32) + norm_back(acc_v[rows], gain, hat, scale)
            acc_v[rows] = value
            go_v[rows] = dot_nt(value.astype(BF), wo_v[...]).astype(BF)
        outs.append(Copy(acc_v, grad_middle, sem()).start())
        outs.append(Copy(go_v, grad_out, sem()).start())
        for copy in later:
            copy.wait()
        prefix_back(q_v, go_v, at_v, to_v, c_v, t_v, gt_v)
        outs.append(Copy(c_v, centres, sem()).start())
        outs.append(Copy(gt_v, grad_table, sem()).start())
        for copy in outs:
            copy.wait()

    return kernel


def feed_back(layer, sec, g, slope, middle, mixed, attended, totals, table, packs, wo, we, wr):
    return call(
        feed_back_kernel(layer),
        (sec, g, slope, middle, mixed, attended, totals, table, *packs, *wo, *we, *wr),
        [SMEM] + [ANY] * 15,
        [
            ((LENGTH, WIDTH), F32), ((LENGTH, WIDTH), BF), ((HEADS, LENGTH), F32),
            ((PAD, 2 * WIDTH), F32),
        ],
        [
            vm((LENGTH, WIDTH)), vm((LENGTH, FF)), vm((LENGTH, WIDTH), F32), vm((LENGTH, WIDTH)),
            vm((LENGTH, WIDTH)), vm((HEADS, LENGTH), F32), vm((PAD, 2 * WIDTH)), vm((16, 1024), F32),
            vm((WIDTH, WIDTH)), vm((WIDTH, FF)), vm((FF, WIDTH)), vm((LENGTH, WIDTH), F32),
            vm((LENGTH, WIDTH)), vm((HEADS, LENGTH), F32), vm((PAD, 2 * WIDTH), F32), DMA((40,)),
        ],
        f"feed_back{layer}", 2 * LENGTH * WIDTH * 9 * WIDTH, 40 << 20,
    )


def attend_back_kernel():
    def kernel(
        sec, lens, mixed, grad_out, totals, centres, table, grad_mixed,
        m_v, go_v, to_v, c_v, t_v, gm_v, k_v, v_v, sems,
    ):
        sem = Sems(sems)
        pairs = ((mixed, m_v), (grad_out, go_v), (totals, to_v), (centres, c_v), (table, t_v))
        copies = [Copy(a, b, sem()).start() for a, b in pairs]
        for copy in copies:
            copy.wait()
        attend_back(m_v, go_v, to_v, c_v, t_v, lens, sec[0], gm_v, (k_v, v_v))
        Copy(gm_v, grad_mixed, sem()).start().wait()

    return kernel


def attend_backward(layer, sec, lens, mixed, grad_out, totals, centres, table):
    return call(
        attend_back_kernel(),
        (sec, lens, mixed, grad_out, totals, centres, table),
        [SMEM, SMEM] + [ANY] * 5,
        [((LENGTH, 3 * WIDTH), BF)],
        [
            vm((LENGTH, 3 * WIDTH)), vm((LENGTH, WIDTH)), vm((HEADS, LENGTH), F32),
            vm((HEADS, LENGTH), F32), vm((PAD, 2 * WIDTH)), vm((LENGTH, 3 * WIDTH)),
            vm((LENGTH, WIDTH), F32), vm((LENGTH, WIDTH), F32), DMA((8,)),
        ],
        f"attend_back{layer}", 2 * LENGTH * WIDTH * 10 * WIDTH, 16 << 20,
    )[0]


def mix_back_kernel(layer):
    def kernel(
        sec, grad_mixed, x, grad_middle, pack, pack2, w, w2, out,
        gm_v, x_v, mid_v, p_v, w_v, o_v, sems,
    ):
        own = sec[0] == layer
        sem = Sems(sems)
        source = x.at[sec[0]] if layer == 0 else x
        gms = [
            Copy(grad_mixed.at[tile(r, 256)], gm_v.at[tile(r, 256)], sem()).start()
            for r in range(1)
        ]
        ws = Copy(w, w_v, sem(), w2, own).start()
        gms += [
            Copy(grad_mixed.at[tile(r, 256)], gm_v.at[tile(r, 256)], sem()).start()
            for r in range(1, 4)
        ]
        packs = Copy(pack, p_v, sem(), pack2, own).start()
        xs = Copy(source, x_v, sem()).start()
        mids = Copy(grad_middle, mid_v, sem()).start()
        ws.wait()
        outs = []
        for r in range(4):
            rows = tile(r, 256)
            gms[r].wait()
            value = dot_nt(gm_v[rows], w_v[...])
            if r == 0:
                packs.wait()
                xs.wait()
                mids.wait()
            hat, scale = normalise(x_v[rows].astype(F32))
            value = mid_v[rows] + norm_back(value, p_v[GAIN_A : GAIN_A + 1], hat, scale)
            o_v[rows] = value.astype(BF)
            outs.append(Copy(o_v.at[rows], out.at[rows], sem()).start())
        for copy in outs:
            copy.wait()

    return kernel


def mix_back(layer, sec, grad_mixed, x, grad_middle, packs, weights):
    return call(
        mix_back_kernel(layer),
        (sec, grad_mixed, x, grad_middle, *packs, *weights),
        [SMEM] + [ANY] * 7,
        [((LENGTH, WIDTH), BF)],
        [
            vm((LENGTH, 3 * WIDTH)), vm((LENGTH, WIDTH)), vm((LENGTH, WIDTH), F32),
            vm((16, 1024), F32), vm((WIDTH, 3 * WIDTH)), vm((LENGTH, WIDTH)), DMA((16,)),
        ],
        f"mix_back{layer}", 2 * LENGTH * WIDTH * 3 * WIDTH, 20 << 20,
    )[0]


def prefix_kernel(count):
    def kernel(table, mine, weight, activity, embed, hidden, ge, gw, gb, gpw, gpb):
        total = jnp.zeros((PAD, activity.shape[1]), F32)
        for index in range(count):
            high, low = split(table[index])
            total = total + dot_nt(high, weight[index]) + dot_nt(low, weight[index])
        act = activity[...]
        pre = total * (1.0 - act * act)
        real = lax.broadcasted_iota(jnp.int32, pre.shape, 0) < PRE
        pre = jnp.where(real, pre, 0.0)
        high, low = split(pre)
        gb[...] = jnp.sum(pre, axis=0, keepdims=True)
        gw[...] = dot_tn(embed[...], high) + dot_tn(embed[...], low)
        ge[...] = dot_nt(high, hidden[...]) + dot_nt(low, hidden[...])
        part = mine[...]
        part = jnp.where(lax.broadcasted_iota(jnp.int32, part.shape, 0) < PRE, part, 0.0)
        high, low = split(part)
        rounded = act.astype(BF)
        gpw[...] = dot_tn(rounded, high) + dot_tn(rounded, low)
        gpb[...] = jnp.sum(part, axis=0, keepdims=True)

    return kernel


def prefix_grads(table, mine, weight, activity, embed, hidden):
    count, _, part = table.shape
    size = activity.shape[1]
    return call(
        prefix_kernel(count),
        (table, mine, weight, activity, embed, hidden),
        [VMEM] * 6,
        [
            ((PAD, WIDTH), F32), ((WIDTH, size), F32), ((1, size), F32), ((size, part), F32),
            ((1, part), F32),
        ],
        [],
        "prefix_grads", 1 << 30, 10 << 20,
        out_specs=[VMEM] * 5,
    )


def per_device(
    inputs, cotangent, doc_lengths, attend_gain, attend_bias, mixing_weight, mixing_bias,
    output_weight, output_bias, feed_gain, feed_bias, expand_weight, expand_bias, reduce_weight,
    reduce_bias, prefix_embed, hidden_weight, hidden_bias, prefix_weight, prefix_bias,
):
    section = lax.axis_index("section")
    sec = section.astype(jnp.int32).reshape(1)
    everyone = ("section", "dp")
    places = lax.axis_size("dp")
    swap = lambda value: lax.ppermute(value, "section", [(0, 1), (1, 0)])
    x = inputs.reshape(2, LENGTH, WIDTH)
    cot = cotangent.reshape(2, LENGTH, WIDTH)
    lens = doc_lengths.reshape(2, DOCS)

    wm = mixing_weight[0]
    wm2 = swap(wm)
    vectors = (
        attend_gain, attend_bias, mixing_bias, output_bias, feed_gain, feed_bias, expand_bias,
        reduce_bias,
    )
    pack = jnp.concatenate([v.astype(F32).reshape(-1, 1024) for v in vectors], 0)
    pack = jnp.pad(pack, ((0, 16 - pack.shape[0]), (0, 0)))
    pack2 = swap(pack)
    packs = (pack, pack2)

    activity = jnp.tanh(
        jnp.dot(prefix_embed, hidden_weight, preferred_element_type=F32) + hidden_bias
    )
    part = (
        jnp.dot(activity.astype(BF), prefix_weight[0], preferred_element_type=F32)
        + prefix_bias[0]
    ).astype(BF)
    part = jnp.pad(part, ((0, PAD - PRE), (0, 0))).astype(F32)
    tables = lax.all_to_all(
        jnp.broadcast_to(part[None], (2 * places, *part.shape)), everyone, 0, 0
    )
    tables = tables.reshape(2, places, PAD, -1).transpose(0, 2, 1, 3).reshape(2, PAD, 2 * WIDTH)
    tables = tables.astype(BF)
    full_prefix = lax.all_gather(prefix_weight[0], everyone, axis=0)

    wo, we = output_weight[0], expand_weight[0]
    wr = reduce_weight[0]
    wo_in, we_in, wm2 = lax.optimization_barrier((wo, we, wm2))
    wo2, we2 = swap(wo_in), swap(we_in)
    wms, wos, wes = (wm, wm2), (wo, wo2), (we, we2)

    kept = []
    hidden = x
    wrs = None
    for layer in range(2):
        mixed = mix(layer, sec, hidden, packs, wms)
        if wrs is None:
            wr_in, mixed = lax.optimization_barrier((wr, mixed))
            wrs = (wr, swap(wr_in))
        attended, totals, middle, slope, active = attend_expand(
            layer, sec, lens, hidden, mixed, tables[layer], packs, wos, wes
        )
        out = reduce(layer, sec, active, middle, packs, wrs)
        kept.append((hidden, mixed, attended, totals, middle, slope))
        hidden = out
        kept[-1] += (out,)
    out0, out1 = kept[0][-1], kept[1][-1]
    from_second = lax.ppermute(out0, "section", [(1, 0)])
    from_first = lax.ppermute(out1, "section", [(0, 1)])

    grad = cot
    grads, table_grads = [None, None], [None, None]
    for layer in (1, 0):
        before, mixed, attended, totals, middle, slope, _ = kept[layer]
        grad_middle, grad_out, centres, table_grads[layer] = feed_back(
            layer, sec, grad, slope, middle, mixed, attended, totals, tables[layer], packs,
            wos, wes, wrs,
        )
        grad_mixed = attend_backward(
            layer, sec, lens, mixed, grad_out, totals, centres, tables[layer]
        )
        grad = mix_back(layer, sec, grad_mixed, before, grad_middle, packs, wms)
        grads[layer] = grad
    grad_second = lax.ppermute(grads[0], "section", [(1, 0)])
    grad_first = lax.ppermute(grads[1], "section", [(0, 1)])

    def both(first, second, other_second, other_first):
        low = jnp.where(section == 0, first, other_first)
        high = jnp.where(section == 0, other_second, second)
        return jnp.stack([low, high])[None, :, None]

    layer_out = both(out0, out1, from_second, from_first)
    input_grad = both(grads[0], grads[1], grad_second, grad_first)

    send = jnp.stack(table_grads).reshape(2, PAD, places, -1).transpose(0, 2, 1, 3)
    send = send.reshape(2 * places, PAD, -1)
    mine = jnp.sum(lax.all_to_all(send, everyone, 0, 0), axis=0)
    summed = lax.all_to_all(
        jnp.broadcast_to(mine[None], (2 * places, *mine.shape)), everyone, 0, 0
    )
    pad_rows = ((0, PAD - PRE), (0, 0))
    ge, gw, gb, gpw, gpb = prefix_grads(
        summed, mine, full_prefix, jnp.pad(activity, pad_rows), jnp.pad(prefix_embed, pad_rows),
        hidden_weight,
    )
    return (layer_out, input_grad, ge[:PRE], gw, gb[0], gpw[None], gpb)


def solution(mesh):
    in_specs = (
        P(None, "dp", None, None),
        P(None, "dp", None, None),
        P(None, "dp", None),
        P("section", None),
        P("section", None),
        P("section", None, None),
        P("section", None),
        P("section", None, None),
        P("section", None),
        P("section", None),
        P("section", None),
        P("section", None, None),
        P("section", None),
        P("section", None, None),
        P("section", None),
        P(),
        P(),
        P(),
        P("section", None, "dp"),
        P("section", "dp"),
    )
    out_specs = (
        P("section", None, "dp", None, None),
        P("section", None, "dp", None, None),
        P(),
        P(),
        P(),
        P("section", None, "dp"),
        P("section", "dp"),
    )
    return jax.shard_map(
        per_device, mesh=mesh, in_specs=in_specs, out_specs=out_specs, check_vma=False
    )
```

time: 1730 us -> 407 us (0.24)
  matrix products: 657 us -> 0.39 us
  waiting for transfers between devices: 443 us -> 36.4 us
  other arithmetic: 304 us -> 12.8 us
  Pallas kernels: 0 us -> 287 us
  local copies, waits for them, and re-layouts: 191 us -> 12.1 us
  blocking collectives: 83.5 us -> 0 us
    dot_general x58 -> x2, matrix products: 657 us -> 0.39 us  [the longest x1 0.26 us: per_device(): jnp.dot(prefix_embed, hidden_weight, preferred_element_type=F32)]
    pallas_call x0 -> x13, Pallas kernels: none -> 287 us  [call(): pl.pallas_call(kernel, in_specs=in_specs, out_specs=out_specs or [ANY] *...]
    reduce_scatter x1 -> x0, waiting for transfers between devices: 268 us -> none  [per_device(): lax.psum_scatter(prefix_total, 'dp', scatter_dimension=1, tiled=True)]
    ppermute x4 -> x9, waiting for transfers between devices: 175 us -> 20.1 us  [the longest x5 20 us: per_device(): swap = lambda value: lax.ppermute(value, 'section', [(0, 1), (1, 0)])]
    reduce_sum x27 -> x1, other arithmetic: 117 us -> 0.04 us  [per_device(): mine = jnp.sum(lax.all_to_all(send, everyone, 0, 0), axis=0)]
    convert_element_type x37 -> x1, other arithmetic: 101 us -> 0.01 us  [per_device(): jnp.dot(prefix_embed, hidden_weight, preferred_element_type=F32)]
    slice x36 -> x3, local copies, waits for them, and re-layouts: 51.5 us -> 0.05 us  [per_device(): tables[layer]]
    concatenate x20 -> x1, local copies, waits for them, and re-layouts: 52.4 us -> 1.5 us  [per_device(): jnp.concatenate([v.astype(F32).reshape(-1, 1024) for v in vectors], 0)]
  transfers between devices with their start and end apart: 5 -> 13, of which waited for: 3 -> 4; matrix products, arithmetic and copies ran while one was open for 11% -> 4% of each run, Pallas kernels for 0% -> 72%
where the time goes in v1:
time: 407 us; the launch traced here: 399 us
  Pallas kernels  287 us (71%)
  waiting for transfers between devices  36.4 us (9%)
  starting transfers between devices  35.4 us (9%)
  between operations  14.6 us (4%)
  other arithmetic  12.8 us (3%)
  local copies, waits for them, and re-layouts  12.1 us (3%)
    pallas_call x13, Pallas kernels, call(): pl.pallas_call(kernel, in_specs=in_specs, out_specs=out_specs or [ANY] *...  287 us
    ppermute x5, waiting for transfers between devices, per_device(): swap = lambda value: lax.ppermute(value, 'section', [(0, 1), (1, 0)])  20 us
    all_to_all x1, waiting for transfers between devices, per_device(): lax.all_to_all(jnp.broadcast_to(mine[None], (2 * places, *mine.shape)), e...  9.29 us
    all_to_all x1, starting transfers between devices, per_device(): mine = jnp.sum(lax.all_to_all(send, everyone, 0, 0), axis=0)  8.48 us
  transfers between devices with their start and end apart: 13, of which 4 were waited for; matrix products, arithmetic and copies ran while one was open for 4% of the time, Pallas kernels for 72%

profile of v1, /device:TPU:1, one launch (start us, length us, event | category | flops | bytes accessed | tf_op | source)
XLA Modules:
  0.0 399.1 jit_solution(15587353326341170197)
XLA Ops:
  7.2 0.1 collective-permute-start.1
  7.3 10.4 %collective-permute-done.1.w2 = bf16[1024,3072]{1,0:T(8,128)(2,1)} collective-permute-done((bf16[1024,3072]{1,0:T(8,128)(2,1)}, bf16[1024,3072]{1,0:T(8,128)(2,1)}, u32[]{:S(2)}, u32[]{:S(2)}) %collective-permute-start.1) | collective-permute-done | bytes 6291488 | tf_op jit(solution)/shard_map/ppermute | solution.py:720
  17.7 0.1 collective-permute-start.3
  17.9 0.7 reduce
  18.6 0.8 reduce.1
  19.4 1.5 concatenate.5
  20.9 0.0 copy-start.5
  20.9 0.4 collective-permute-start
  21.4 9.6 %collective-permute-done.pack2 = f32[16,1024]{1,0:T(8,128)S(1)} collective-permute-done((f32[16,1024]{1,0:T(8,128)S(1)}, f32[16,1024]{1,0:T(8,128)S(1)}, u32[]{:S(2)}, u32[]{:S(2)}) %collective-permute-start) | collective-permute-done | bytes 65568 | tf_op jit(solution)/shard_map/ppermute | solution.py:720
  31.0 0.6 copy-done.9
  31.6 0.0 copy-start.6
  31.6 12.5 %mix0.1.mixed = bf16[1024,3072]{1,0:T(8,128)(2,1)} custom-call(s32[1]{0:T(128)} %bitcast.sec, bf16[2,1024,1024]{2,1,0:T(8,128)(2,1)} %bitcast.62, f32[16,1024]{1,0:T(8,128)} %copy-done.5, f32[16,1024]{1,0:T(8,128)} %copy-done.9, bf16[1024,3072]{1,0:T(8,128)(2,1)} %bitcast.58, bf16[1024,3072]{1,0:T(8,128)(2,1)} %collective-permute-done.1.w2), custom_call_target="tpu_custom_call" | custom-call | flops 6442450944 | bytes 14680064 | tf_op jit(solution)/shard_map/mix0/pallas_call | solution.py:48
  44.1 0.2 collective-permute-start.4
  44.3 0.4 collective-permute-start.2
  44.7 0.3 fusion
  45.0 0.1 fusion.1
  45.2 0.5 copy-done.7
  45.6 0.7 broadcast_in_dim.10
  46.3 7.1 %all-to-all-start = ((bf16[32,16,128]{2,1,0:T(8,128)(2,1)}), bf16[32,16,128]{2,1,0:T(8,128)(2,1)S(1)}, u32[]{:S(2)}, u32[]{:S(2)}) async-start(bf16[32,16,128]{2,1,0:T(8,128)(2,1)} %broadcast_in_dim.10), calls=%async_computation | async-start | bytes 262144 | tf_op jit(solution)/shard_map/all_to_all | solution.py:744
  53.4 0.5 all-gather.2.cloned.1.call-start
  53.9 0.2 all-gather.2.cloned.1.call-update
  54.1 6.9 %all-to-all-done = bf16[32,16,128]{2,1,0:T(8,128)(2,1)S(1)} async-done(((bf16[32,16,128]{2,1,0:T(8,128)(2,1)}), bf16[32,16,128]{2,1,0:T(8,128)(2,1)S(1)}, u32[]{:S(2)}, u32[]{:S(2)}) %all-to-all-start) | async-done | bytes 131104 | tf_op jit(solution)/shard_map/all_to_all | solution.py:744
  61.0 0.6 copy.48
  61.7 0.6 copy.47
  62.3 1.3 copy-done.14
  63.6 38.9 %attend_expand0.1 = (bf16[1024,1024]{1,0:T(8,128)(2,1)}, f32[16,1024]{1,0:T(8,128)}, f32[1024,1024]{1,0:T(8,128)}, bf16[1024,4096]{1,0:T(8,128)(2,1)}, bf16[1024,4096]{1,0:T(8,128)(2,1)}) custom-call(s32[1]{0:T(128)} %bitcast.sec, s32[2,8]{1,0:T(2,128)} %bitcast.97, bf16[2,1024,1024]{2,1,0:T(8,128)(2,1)} %bitcast.63, bf16[1024,3072]{1,0:T(8,128)(2,1)} %mix0.1.mixed, ...), custom_call_target="tpu_custom_call" | custom-call | flops 17179869184 | bytes 46137344 | tf_op jit(solution)/shard_map/attend_expand0/pallas_call | solution.py:48
  102.5 0.0 collective-permute-done.4.wr2
  102.6 17.1 %reduce0.1.x = bf16[1024,1024]{1,0:T(8,128)(2,1)} custom-call(s32[1]{0:T(128)} %bitcast.sec, bf16[1024,4096]{1,0:T(8,128)(2,1)} %get-tuple-element.39.active, f32[1024,1024]{1,0:T(8,128)} %get-tuple-element.40.middle, f32[16,1024]{1,0:T(8,128)} %copy-done.5, f32[16,1024]{1,0:T(8,128)} %copy-done.9, bf16[4096,1024]{1,0:T(8,128)(2,1)} %bitcast.84, ...), custom_call_target="tpu_custom_call" | custom-call | flops 8589934592 | bytes 23068672 | tf_op jit(solution)/shard_map/reduce0/pallas_call | solution.py:48
  119.6 4.0 %collective-permute-start.6 = (bf16[1024,1024]{1,0:T(8,128)(2,1)}, bf16[1024,1024]{1,0:T(8,128)(2,1)}, u32[]{:S(2)}, u32[]{:S(2)}) collective-permute-start(bf16[1024,1024]{1,0:T(8,128)(2,1)} %reduce0.1.x), channel_id=1, source_target_pairs={{16,0},{17,1},{18,2},{19,3},{20,4},{21,5},{22,6},{23,7},{24,8},{25... | collective-permute-start | bytes 6291464 | tf_op jit(solution)/shard_map/ppermute | solution.py:773
  123.7 12.3 %mix1.1.mixed = bf16[1024,3072]{1,0:T(8,128)(2,1)} custom-call(s32[1]{0:T(128)} %bitcast.sec, bf16[1024,1024]{1,0:T(8,128)(2,1)} %reduce0.1.x, f32[16,1024]{1,0:T(8,128)} %copy-done.5, f32[16,1024]{1,0:T(8,128)} %copy-done.9, bf16[1024,3072]{1,0:T(8,128)(2,1)} %bitcast.59, bf16[1024,3072]{1,0:T(8,128)(2,1)} %collective-permute-done.1.w2), custom_call_target="tpu_custom_call" | custom-call | flops 6442450944 | bytes 14680064 | tf_op jit(solution)/shard_map/mix1/pallas_call | solution.py:48
  136.0 38.7 %attend_expand1.1 = (bf16[1024,1024]{1,0:T(8,128)(2,1)}, f32[16,1024]{1,0:T(8,128)}, f32[1024,1024]{1,0:T(8,128)}, bf16[1024,4096]{1,0:T(8,128)(2,1)}, bf16[1024,4096]{1,0:T(8,128)(2,1)}) custom-call(s32[1]{0:T(128)} %bitcast.sec, s32[2,8]{1,0:T(2,128)} %bitcast.98, bf16[1024,1024]{1,0:T(8,128)(2,1)} %reduce0.1.x, bf16[1024,3072]{1,0:T(8,128)(2,1)} %mix1.1.mixed, ...), custom_call_target="tpu_custom_call" | custom-call | flops 17179869184 | bytes 46137344 | tf_op jit(solution)/shard_map/attend_expand1/pallas_call | solution.py:48
  174.7 17.0 %reduce1.1 = bf16[1024,1024]{1,0:T(8,128)(2,1)} custom-call(s32[1]{0:T(128)} %bitcast.sec, bf16[1024,4096]{1,0:T(8,128)(2,1)} %get-tuple-element.42.active, f32[1024,1024]{1,0:T(8,128)} %get-tuple-element.43.middle, f32[16,1024]{1,0:T(8,128)} %copy-done.5, f32[16,1024]{1,0:T(8,128)} %copy-done.9, bf16[4096,1024]{1,0:T(8,128)(2,1)} %bitcast.85, ...), custom_call_target="tpu_custom_call" | custom-call | flops 8589934592 | bytes 23068672 | tf_op jit(solution)/shard_map/reduce1/pallas_call | solution.py:48
  191.7 1.5 collective-permute-start.5
  193.2 30.7 %feed_back1.1 = (f32[1024,1024]{1,0:T(8,128)}, bf16[1024,1024]{1,0:T(8,128)(2,1)}, f32[16,1024]{1,0:T(8,128)}, f32[16,2048]{1,0:T(8,128)}) custom-call(s32[1]{0:T(128)} %bitcast.sec, bf16[2,1024,1024]{2,1,0:T(8,128)(2,1)} %bitcast.88, bf16[1024,4096]{1,0:T(8,128)(2,1)} %get-tuple-element.44.slope, f32[1024,1024]{1,0:T(8,128)} %get-tuple-element.43.middle, ...), custom_call_target="tpu_custom_call" | custom-call | flops 19327352832 | bytes 41943040 | tf_op jit(solution)/shard_map/feed_back1/pallas_call | solution.py:48
  224.0 0.9 copy.44
  225.0 26.9 %attend_back1.1.grad_mixed = bf16[1024,3072]{1,0:T(8,128)(2,1)} custom-call(s32[1]{0:T(128)} %bitcast.sec, s32[2,8]{1,0:T(2,128)} %bitcast.99, bf16[1024,3072]{1,0:T(8,128)(2,1)} %mix1.1.mixed, bf16[1024,1024]{1,0:T(8,128)(2,1)} %get-tuple-element.47.grad_out, f32[16,1024]{1,0:T(8,128)} %get-tuple-element.46.totals, f32[16,1024]{1,0:T(8,128)} %get-tuple-element.48.centres, ...), custom_call_target="tpu_custom_call" | custom-call | flops 21474836480 | bytes 16777216 | tf_op jit(solution)/shard_map/attend_back1/pallas_call | solution.py:48
  251.8 14.3 %mix_back1.1.g = bf16[1024,1024]{1,0:T(8,128)(2,1)} custom-call(s32[1]{0:T(128)} %bitcast.sec, bf16[1024,3072]{1,0:T(8,128)(2,1)} %attend_back1.1.grad_mixed, bf16[1024,1024]{1,0:T(8,128)(2,1)} %reduce0.1.x, f32[1024,1024]{1,0:T(8,128)} %get-tuple-element.49.grad_middle, f32[16,1024]{1,0:T(8,128)} %copy-done.5, f32[16,1024]{1,0:T(8,128)} %copy-done.9, ...), custom_call_target="tpu_custom_call" | custom-call | flops 6442450944 | bytes 20971520 | tf_op jit(solution)/shard_map/mix_back1/pallas_call | solution.py:48
  266.2 30.5 %feed_back0.1 = (f32[1024,1024]{1,0:T(8,128)}, bf16[1024,1024]{1,0:T(8,128)(2,1)}, f32[16,1024]{1,0:T(8,128)}, f32[16,2048]{1,0:T(8,128)}) custom-call(s32[1]{0:T(128)} %bitcast.sec, bf16[1024,1024]{1,0:T(8,128)(2,1)} %mix_back1.1.g, bf16[1024,4096]{1,0:T(8,128)(2,1)} %get-tuple-element.50.slope, f32[1024,1024]{1,0:T(8,128)} %get-tuple-element.40.middle, ...), custom_call_target="tpu_custom_call" | custom-call | flops 19327352832 | bytes 41943040 | tf_op jit(solution)/shard_map/feed_back0/pallas_call | solution.py:48
  296.7 0.9 copy.43
  297.7 0.7 pad_maximum_fusion
  298.4 8.5 %all-to-all-start.1 = ((f32[32,16,128]{2,1,0:T(8,128)}), f32[32,16,128]{2,1,0:T(8,128)S(1)}, u32[]{:S(2)}, u32[]{:S(2)}) async-start(f32[32,16,128]{2,1,0:T(8,128)} %bitcast.22), calls=%async_computation.1 | async-start | bytes 524288 | tf_op jit(solution)/shard_map/all_to_all | solution.py:802
  306.9 26.8 %attend_back0.1.grad_mixed = bf16[1024,3072]{1,0:T(8,128)(2,1)} custom-call(s32[1]{0:T(128)} %bitcast.sec, s32[2,8]{1,0:T(2,128)} %bitcast.100, bf16[1024,3072]{1,0:T(8,128)(2,1)} %mix0.1.mixed, bf16[1024,1024]{1,0:T(8,128)(2,1)} %get-tuple-element.53.grad_out, f32[16,1024]{1,0:T(8,128)} %get-tuple-element.52.totals, f32[16,1024]{1,0:T(8,128)} %get-tuple-element.54.centres, ...), custom_call_target="tpu_custom_call" | custom-call | flops 21474836480 | bytes 16777216 | tf_op jit(solution)/shard_map/attend_back0/pallas_call | solution.py:48
  333.8 0.0 copy-start.11
  333.8 14.5 %mix_back0.1 = bf16[1024,1024]{1,0:T(8,128)(2,1)} custom-call(s32[1]{0:T(128)} %bitcast.sec, bf16[1024,3072]{1,0:T(8,128)(2,1)} %attend_back0.1.grad_mixed, bf16[2,1024,1024]{2,1,0:T(8,128)(2,1)} %bitcast.64, f32[1024,1024]{1,0:T(8,128)} %get-tuple-element.55.grad_middle, f32[16,1024]{1,0:T(8,128)} %copy-done.5, f32[16,1024]{1,0:T(8,128)} %copy-done.9, ...), custom_call_target="tpu_custom_call" | custom-call | flops 6442450944 | bytes 20971520 | tf_op jit(solution)/shard_map/mix_back0/pallas_call | solution.py:48
  348.3 3.5 collective-permute-start.8
  351.7 1.3 collective-permute-start.7
  353.1 0.7 broadcast_in_dim.26
  353.8 7.7 %all-to-all-start.2 = ((f32[32,16,128]{2,1,0:T(8,128)}), f32[32,16,128]{2,1,0:T(8,128)S(1)}, u32[]{:S(2)}, u32[]{:S(2)}) async-start(f32[32,16,128]{2,1,0:T(8,128)} %broadcast_in_dim.26), calls=%async_computation.2 | async-start | bytes 524288 | tf_op jit(solution)/shard_map/all_to_all | solution.py:803
  361.6 0.6 pad.21.activity
  362.2 0.6 pad.22.embed
  362.8 9.3 %all-to-all-done.2.table = f32[32,16,128]{2,1,0:T(8,128)S(1)} async-done(((f32[32,16,128]{2,1,0:T(8,128)}), f32[32,16,128]{2,1,0:T(8,128)S(1)}, u32[]{:S(2)}, u32[]{:S(2)}) %all-to-all-start.2) | async-done | bytes 262176 | tf_op jit(solution)/shard_map/all_to_all | solution.py:803
  372.1 0.7 copy-done.4
  372.8 7.1 %prefix_grads.1 = (f32[16,1024]{1,0:T(8,128)}, f32[1024,512]{1,0:T(8,128)}, f32[1,512]{1,0:T(1,128)}, f32[512,128]{1,0:T(8,128)}, f32[1,128]{1,0:T(1,128)}) custom-call(f32[32,16,128]{2,1,0:T(8,128)} %copy-done.4, f32[16,128]{1,0:T(8,128)} %copy-done.12, bf16[32,512,128]{2,1,0:T(8,128)(2,1)} %all-gather.2.cloned.1.call-done.weight, f32[16,512]{1,0:T(8,128)} %pad.21.activity, ...), custom_call_target="tpu_custom_call" | custom-call | flops 1073741824 | bytes 10485760 | tf_op jit(solution)/shard_map/prefix_grads/pallas_call | solution.py:48
  379.9 0.0 collective-permute-done.6
  379.9 2.0 select_bitcast_fusion.2
  381.8 0.0 collective-permute-done.5
  381.8 0.2 copy-done
  382.1 1.8 select_bitcast_fusion.3
  383.9 2.4 maximum_bitcast_fusion
  386.3 0.0 collective-permute-done.8
  386.3 0.2 select_bitcast_fusion
  386.5 1.4 copy-done.2
  387.9 1.8 select_bitcast_fusion.1
  389.7 2.4 maximum_bitcast_fusion.1
  (40 shorter events, 0.3 us)
Async XLA Ops:
  7.2 10.6 %collective-permute-start.1 = (bf16[1024,3072]{1,0:T(8,128)(2,1)}, bf16[1024,3072]{1,0:T(8,128)(2,1)}, u32[]{:S(2)}, u32[]{:S(2)}) collective-permute-start(bf16[1024,3072]{1,0:T(8,128)(2,1)} %bitcast.57), channel_id=1, source_target_pairs={{0,16},{16,0},{1,17},{17,1},{2,18},{18,2},{3,19},{19,3},{4,20},{20... | collective-permute-start | bytes 18874376 | tf_op jit(solution)/shard_map/ppermute | solution.py:720
  17.7 44.6 %collective-permute-start.3 = (bf16[1024,4096]{1,0:T(8,128)(2,1)}, bf16[1024,4096]{1,0:T(8,128)(2,1)}, u32[]{:S(2)}, u32[]{:S(2)}) collective-permute-start(bf16[1024,4096]{1,0:T(8,128)(2,1)} %bitcast.78), channel_id=1, source_target_pairs={{0,16},{16,0},{1,17},{17,1},{2,18},{18,2},{3,19},{19,3},{4,20},{20... | collective-permute-start | bytes 25165832 | tf_op jit(solution)/shard_map/ppermute | solution.py:720
  20.9 10.1 %copy-start.5 = (f32[16,1024]{1,0:T(8,128)}, f32[16,1024]{1,0:T(8,128)S(1)}, u32[]{:S(2)}) copy-start(f32[16,1024]{1,0:T(8,128)S(1)} %pad_convert_fusion.pack) | copy-start | bytes 196612
  20.9 10.0 %collective-permute-start = (f32[16,1024]{1,0:T(8,128)S(1)}, f32[16,1024]{1,0:T(8,128)S(1)}, u32[]{:S(2)}, u32[]{:S(2)}) collective-permute-start(f32[16,1024]{1,0:T(8,128)S(1)} %pad_convert_fusion.pack), channel_id=1, source_target_pairs={{0,16},{16,0},{1,17},{17,1},{2,18},{18,2},{3,19},{19,3},{4,20},{20... | collective-permute-start | bytes 196616 | tf_op jit(solution)/shard_map/ppermute | solution.py:720
  31.0 0.6 copy-start.9
  31.6 13.1 %copy-start.13 = (bf16[512]{0:T(512)(128)(2,1)S(1)}, bf16[512]{0:T(512)(128)(2,1)}, u32[]{:S(2)}) copy-start(bf16[512]{0:T(512)(128)(2,1)} %param.37) | copy-start | bytes 3076
  31.6 13.1 %copy-start.15 = (bf16[1,128]{1,0:T(2,128)(2,1)S(1)}, bf16[1,128]{1,0:T(2,128)(2,1)}, u32[]{:S(2)}) copy-start(bf16[1,128]{1,0:T(2,128)(2,1)} %param.39) | copy-start | bytes 772
  31.6 13.1 %copy-start.3 = (bf16[1024,512]{1,0:T(8,128)(2,1)S(1)}, bf16[1024,512]{1,0:T(8,128)(2,1)}, u32[]{:S(2)}) copy-start(bf16[1024,512]{1,0:T(8,128)(2,1)} %hidden.1) | copy-start | bytes 3145732
  31.6 13.1 %copy-start.10 = (bf16[10,1024]{1,0:T(8,128)(2,1)S(1)}, bf16[10,1024]{1,0:T(8,128)(2,1)}, u32[]{:S(2)}) copy-start(bf16[10,1024]{1,0:T(8,128)(2,1)} %param.35) | copy-start | bytes 61444
  31.6 13.4 %copy-start.6 = (bf16[1,512,128]{2,1,0:T(8,128)(2,1)S(1)}, bf16[1,512,128]{2,1,0:T(8,128)(2,1)}, u32[]{:S(2)}) copy-start(bf16[1,512,128]{2,1,0:T(8,128)(2,1)} %param.38) | copy-start | bytes 393220
  44.1 58.4 %collective-permute-start.4 = (bf16[4096,1024]{1,0:T(8,128)(2,1)}, bf16[4096,1024]{1,0:T(8,128)(2,1)}, u32[]{:S(2)}, u32[]{:S(2)}) collective-permute-start(bf16[4096,1024]{1,0:T(8,128)(2,1)} %bitcast.83), channel_id=1, source_target_pairs={{0,16},{16,0},{1,17},{17,1},{2,18},{18,2},{3,19},{19,3},{4,20},{20... | collective-permute-start | bytes 25165832 | tf_op jit(solution)/shard_map/ppermute | solution.py:720
  44.3 18.0 %collective-permute-start.2 = (bf16[1024,1024]{1,0:T(8,128)(2,1)}, bf16[1024,1024]{1,0:T(8,128)(2,1)S(1)}, u32[]{:S(2)}, u32[]{:S(2)}) collective-permute-start(bf16[1024,1024]{1,0:T(8,128)(2,1)} %bitcast.89), channel_id=1, source_target_pairs={{0,16},{16,0},{1,17},{17,1},{2,18},{18,2},{3,19},{19,3},{4,20},{20... | collective-permute-start | bytes 6291464 | tf_op jit(solution)/shard_map/ppermute | solution.py:720
  45.0 0.6 copy-start.7
  46.3 14.7 %all-to-all-start = ((bf16[32,16,128]{2,1,0:T(8,128)(2,1)}), bf16[32,16,128]{2,1,0:T(8,128)(2,1)S(1)}, u32[]{:S(2)}, u32[]{:S(2)}) async-start(bf16[32,16,128]{2,1,0:T(8,128)(2,1)} %broadcast_in_dim.10), calls=%async_computation | async-start | bytes 262144 | tf_op jit(solution)/shard_map/all_to_all | solution.py:744
  53.4 309.4 %all-gather.2.cloned.1.call-start = ((), (), s32[]{:S(2)}) async-start(), calls=%async_computation.3 | async-start | bytes 4325376 | tf_op jit(solution)/shard_map/all_gather | solution.py:749
  62.3 1.3 copy-start.14
  119.6 260.2 %collective-permute-start.6 = (bf16[1024,1024]{1,0:T(8,128)(2,1)}, bf16[1024,1024]{1,0:T(8,128)(2,1)}, u32[]{:S(2)}, u32[]{:S(2)}) collective-permute-start(bf16[1024,1024]{1,0:T(8,128)(2,1)} %reduce0.1.x), channel_id=1, source_target_pairs={{16,0},{17,1},{18,2},{19,3},{20,4},{21,5},{22,6},{23,7},{24,8},{25... | collective-permute-start | bytes 6291464 | tf_op jit(solution)/shard_map/ppermute | solution.py:773
  191.7 190.1 %collective-permute-start.5 = (bf16[1024,1024]{1,0:T(8,128)(2,1)}, bf16[1024,1024]{1,0:T(8,128)(2,1)}, u32[]{:S(2)}, u32[]{:S(2)}) collective-permute-start(bf16[1024,1024]{1,0:T(8,128)(2,1)} %reduce1.1), channel_id=1, source_target_pairs={{0,16},{1,17},{2,18},{3,19},{4,20},{5,21},{6,22},{7,23},{8,24},{9,... | collective-permute-start | bytes 6291464 | tf_op jit(solution)/shard_map/ppermute | solution.py:774
  298.4 54.6 %all-to-all-start.1 = ((f32[32,16,128]{2,1,0:T(8,128)}), f32[32,16,128]{2,1,0:T(8,128)S(1)}, u32[]{:S(2)}, u32[]{:S(2)}) async-start(f32[32,16,128]{2,1,0:T(8,128)} %bitcast.22), calls=%async_computation.1 | async-start | bytes 524288 | tf_op jit(solution)/shard_map/all_to_all | solution.py:802
  333.8 18.0 %copy-start.1 = (bf16[1024,1024]{1,0:T(8,128)(2,1)S(1)}, bf16[1024,1024]{1,0:T(8,128)(2,1)}, u32[]{:S(2)}) copy-start(bf16[1024,1024]{1,0:T(8,128)(2,1)} %mix_back1.1.g) | copy-start | bytes 6291460
  333.8 27.8 %copy-start.8 = (f32[10,512]{1,0:T(8,128)S(1)}, f32[10,512]{1,0:T(8,128)}, u32[]{:S(2)}) copy-start(f32[10,512]{1,0:T(8,128)} %copy-done.7) | copy-start | bytes 61444
  333.8 28.4 %copy-start.11 = (bf16[10,1024]{1,0:T(8,128)(2,1)S(1)}, bf16[10,1024]{1,0:T(8,128)(2,1)}, u32[]{:S(2)}) copy-start(bf16[10,1024]{1,0:T(8,128)(2,1)} %param.35) | copy-start | bytes 61444
  348.3 38.0 %collective-permute-start.8 = (bf16[1024,1024]{1,0:T(8,128)(2,1)}, bf16[1024,1024]{1,0:T(8,128)(2,1)}, u32[]{:S(2)}, u32[]{:S(2)}) collective-permute-start(bf16[1024,1024]{1,0:T(8,128)(2,1)} %mix_back0.1), channel_id=1, source_target_pairs={{16,0},{17,1},{18,2},{19,3},{20,4},{21,5},{22,6},{23,7},{24,8},{25... | collective-permute-start | bytes 6291464 | tf_op jit(solution)/shard_map/ppermute | solution.py:789
  351.7 34.8 %collective-permute-start.7 = (bf16[1024,1024]{1,0:T(8,128)(2,1)S(1)}, bf16[1024,1024]{1,0:T(8,128)(2,1)}, u32[]{:S(2)}, u32[]{:S(2)}) collective-permute-start(bf16[1024,1024]{1,0:T(8,128)(2,1)S(1)} %copy-done.1), channel_id=1, source_target_pairs={{0,16},{1,17},{2,18},{3,19},{4,20},{5,21},{6,22},{7,23},{8,24},{9,... | collective-permute-start | bytes 6291464 | tf_op jit(solution)/shard_map/ppermute | solution.py:790
  353.1 19.0 %copy-start.12 = (f32[16,128]{1,0:T(8,128)}, f32[16,128]{1,0:T(8,128)S(1)}, u32[]{:S(2)}) copy-start(f32[16,128]{1,0:T(8,128)S(1)} %reduce_sum.9.mine) | copy-start | bytes 24580
  353.8 18.3 %all-to-all-start.2 = ((f32[32,16,128]{2,1,0:T(8,128)}), f32[32,16,128]{2,1,0:T(8,128)S(1)}, u32[]{:S(2)}, u32[]{:S(2)}) async-start(f32[32,16,128]{2,1,0:T(8,128)} %broadcast_in_dim.26), calls=%async_computation.2 | async-start | bytes 524288 | tf_op jit(solution)/shard_map/all_to_all | solution.py:803
  372.1 0.7 copy-start.4
  379.8 2.2 copy-start
  386.3 1.6 copy-start.2
Sparse Core Ops, SparseCore 0:
  57.2 63.3 all-gather.1
